TPU v7x, 768 devices: a whole 4x8x12 slice. The times are simulated.
768 devices in a mesh: seq: 24 (over y, z_lo), tensor: 32 (over z_hi, x, core).
Axes of the slice: x: 4, y: 8, z: 12 (z_hi: 4, z_lo: 3; z = z_hi * 3 + z_lo), core: 2. Of those that a mesh axis runs over, the one named last changes fastest.
Arguments:
- frames: bfloat16 [18432, 1536], P('seq'), may hold values from -6 to 6
- w_up: bfloat16 [1536, 6144], P(None, 'tensor'), may hold values from -0.15625 to 0.15625
- w_down: bfloat16 [6144, 1536], P('tensor'), may hold values from -0.078125 to 0.078125
- kernel: float32 [31, 1536], P(None, 'tensor'), may hold values from -1 to 1
- utt_bounds: int32 [2, 18432], P(None, 'seq'), may hold values from 0 to 18432, as said below
- cotangent: bfloat16 [18432, 1536], P('seq', 'tensor'), may hold values from -6 to 6
Outputs:
- output: bfloat16 [18432, 1536], P('seq', 'tensor')
- grad_w_up: float32 [1536, 6144], P(None, 'tensor')
- grad_w_down: float32 [6144, 1536], P('tensor')
- grad_kernel: float32 [31, 1536], P(None, 'tensor')
Inputs may be any that keep to these rules, and one draw needn't show every extreme that they name: Utterances are contiguous runs of frames; for every frame t, utt_bounds[0, t] <= t < utt_bounds[1, t], and all frames of one utterance carry the same pair. Utterances hold 48 to min(800, 9216) frames, except the last, which the stream's end may cut.
All inputs are finite; a program needn't handle non-finite values.
Results may differ from a plain program's by a relative error of at most 0.0061.
Values may be sent and summed in bfloat16 or wider, within the bound.
A program may use at most 64 MiB of HBM per device.

v0:
```python
import math

import jax
import jax.numpy as jnp
from jax import lax
from jax.sharding import PartitionSpec as P

K = 31


def extended(block, sides, width):
    for axis, dim in sides:
        count = lax.axis_size(axis)
        forward = [(i, i + 1) for i in range(count - 1)]
        backward = [(target, source) for source, target in forward]
        low = lax.ppermute(
            lax.slice_in_dim(block, block.shape[dim] - width, None, axis=dim), axis, forward
        )
        high = lax.ppermute(lax.slice_in_dim(block, 0, width, axis=dim), axis, backward)
        block = jnp.concatenate([low, block, high], axis=dim)
    return block


def in_utterance(lower, upper, spots, offset):
    target = spots + offset
    return ((target >= lower) & (target < upper)).astype(jnp.float32)[None, :]


def body(frames, w_up, w_down, kernel, utt_bounds, cotangent):
    length = frames.shape[0]
    width = kernel.shape[1]
    half = K // 2
    first = lax.axis_index("seq") * length
    position = first + jnp.arange(length, dtype=jnp.int32)
    masks = [in_utterance(utt_bounds[0], utt_bounds[1], position, tap - half) for tap in range(K)]
    wide = frames.astype(jnp.float32)
    mean = jnp.mean(wide, axis=1, keepdims=True)
    centred = wide - mean
    var = jnp.mean(centred * centred, axis=1, keepdims=True)
    normed = (centred / jnp.sqrt(var + 1e-05)).astype(jnp.bfloat16)
    act = jnp.dot(normed, w_up, preferred_element_type=jnp.float32)
    act_sig = jax.nn.sigmoid(act)
    hidden = (act * act_sig).astype(jnp.bfloat16)
    block = w_down
    branch = lax.psum_scatter(
        0.5
        * lax.dot_general(
            block, hidden, (((0,), (1,)), ((), ())), preferred_element_type=jnp.float32
        ),
        "tensor",
        scatter_dimension=0,
        tiled=True,
    )
    column = lax.axis_index("tensor") * width
    own_x = lax.dynamic_slice_in_dim(frames, column, width, 1).astype(jnp.float32).T
    mixed = (own_x + branch).astype(jnp.bfloat16)
    cot_cols = cotangent.T
    glu_source = extended(mixed, (("seq", 1),), half).astype(jnp.float32)
    conv = jnp.zeros((width, length), jnp.float32)
    for tap in range(K):
        conv = conv + kernel[tap][:, None] * glu_source[:, tap : tap + length] * masks[tap]
    conv_sig = jax.nn.sigmoid(conv)
    grad_conv = cot_cols.astype(jnp.float32) * conv_sig * (1.0 + conv * (1.0 - conv_sig))
    grad_source = extended(grad_conv, (("seq", 1),), half)
    output = (mixed.astype(jnp.float32) + conv * conv_sig).astype(jnp.bfloat16).T
    grad_glu = jnp.zeros((width, length), jnp.float32)
    kernel_terms = []
    for tap in range(K):
        mirror = 2 * half - tap
        grad_glu = (
            grad_glu
            + kernel[tap][:, None] * grad_source[:, mirror : mirror + length] * masks[mirror]
        )
        kernel_terms.append(
            jnp.sum(grad_conv * glu_source[:, tap : tap + length] * masks[tap], axis=1)
        )
    grad_mixed = (cot_cols.astype(jnp.float32) + grad_glu).astype(jnp.bfloat16)
    piece = lax.all_gather(grad_mixed, "tensor", axis=0, tiled=True)
    block = w_down
    backward = lax.dot_general(
        piece, block, (((0,), (1,)), ((), ())), preferred_element_type=jnp.float32
    )
    term = lax.dot_general(
        hidden, piece, (((0,), (1,)), ((), ())), preferred_element_type=jnp.float32
    )
    down_total = term
    backward, down_total = (backward, down_total)
    grad_down = 0.5 * down_total
    grad_hidden = 0.5 * backward
    grad_act = (grad_hidden * act_sig * (1.0 + act * (1.0 - act_sig))).astype(jnp.bfloat16)
    grad_kernel = jnp.stack(kernel_terms)
    scale = 1.0 / math.sqrt(length * lax.axis_size("seq"))
    grad_up = lax.dot_general(
        normed, grad_act, (((0,), (0,)), ((), ())), preferred_element_type=jnp.float32
    )
    summed_up, summed_down, summed_kernel = lax.psum((grad_up, grad_down, grad_kernel), "seq")
    return (output, summed_up * scale, summed_down * scale, summed_kernel * scale)


def solution(mesh):
    return jax.shard_map(
        body,
        mesh=mesh,
        in_specs=(
            P("seq", None),
            P(None, "tensor"),
            P("tensor", None),
            P(None, "tensor"),
            P(None, "seq"),
            P("seq", "tensor"),
        ),
        out_specs=(P("seq", "tensor"), P(None, "tensor"), P("tensor", None), P(None, "tensor")),
        check_vma=False,
    )
```

profile of v0, /device:TPU:196, one launch (start us, length us, event | category | flops | bytes accessed | tf_op | source)
XLA Modules:
  0.0 549.4 jit_solution(8190739353001255206)
XLA Ops:
  7.2 0.0 reduce-scatter.4.cloned.1.call-start
  7.2 2.2 convert_reduce_fusion
  9.4 0.2 copy-done.1
  9.6 0.8 fusion.2
  10.4 0.6 fusion.3
  11.0 1.4 copy-done.2
  12.4 0.9 fusion.172
  13.3 0.8 copy-done.4
  14.1 3.0 multiply_bitcast_fusion
  17.2 6.0 %copy.58 = f32[1536,768]{1,0:T(8,128)} copy(f32[1536,768]{0,1:T(8,128)} %multiply_bitcast_fusion) | data formatting | bytes 9437184
  23.2 0.0 reduce-scatter.4.cloned.1.call-update
  23.2 0.0 all-gather.2.cloned.1.call-start
  23.3 0.1 constant_dynamic-slice_fusion
  23.4 0.1 copy.60
  23.5 0.4 copy-done.19
  23.9 0.6 slice_bitcast_fusion.29
  24.5 0.7 slice_bitcast_fusion.30
  25.2 133.4 %reduce-scatter.4.cloned.1.call-done = f32[48,768]{1,0:T(8,128)} async-done(((f32[1536,768]{1,0:T(8,128)}), f32[48,768]{1,0:T(8,128)}) %reduce-scatter.4.cloned.1.call-update) | async-done | bytes 147472 | tf_op jit(solution)/shard_map/reduce_scatter | solution.py:45
  158.6 0.9 fusion.134
  159.6 0.1 fusion.171
  159.6 1.3 collective-permute-start.1
  160.9 5.8 %collective-permute-start = (bf16[48,15]{1,0:T(8,128)(2,1)S(1)}, bf16[48,15]{1,0:T(8,128)(2,1)S(1)}, u32[]{:S(2)}, u32[]{:S(2)}) collective-permute-start(bf16[48,15]{1,0:T(8,128)(2,1)S(1)} %get-tuple-element.84), channel_id=1, source_target_pairs={{0,32},{32,64},{64,96},{96,128},{128,160},{160,192},{192,224},{224... | collective-permute-start | bytes 4328 | tf_op jit(solution)/shard_map/ppermute | solution.py:16
  166.7 0.4 fusion.139
  167.2 0.9 collective-permute-done
  168.1 0.1 maximum_convert_fusion
  168.5 3.6 multiply_reduce_fusion
  172.2 0.1 fusion.170
  172.2 5.4 collective-permute-start.3
  177.6 1.3 collective-permute-start.2
  178.9 0.2 collective-permute-done.3
  179.1 5.4 collective-permute-done.2
  184.9 2.5 fusion.19
  187.4 0.2 all-reduce.3.cloned.1.call-start
  187.6 75.9 %all-gather.2.cloned.1.call-done = bf16[1536,768]{1,0:T(8,128)(2,1)} async-done(((bf16[48,768]{1,0:T(8,128)(2,1)}), bf16[1536,768]{1,0:T(8,128)(2,1)}) %all-gather.2.cloned.1.call-update) | async-done | bytes 2359312 | tf_op jit(solution)/shard_map/all_gather | solution.py:78
  263.5 4.2 fusion.7
  267.7 3.8 convolution_multiply_fusion
  271.6 0.0 all-reduce.3.cloned.1.call-update
  271.6 0.6 copy-done.12
  272.3 0.3 multiply_reduce_fusion.27
  272.6 0.7 multiply_reduce_fusion.18
  273.3 0.7 multiply_reduce_fusion.1
  274.1 0.1 stack.127
  274.1 116.5 %psum.23 = f32[31,48]{1,0:T(8,128)S(1)} all-reduce(f32[31,48]{1,0:T(8,128)S(1)} %stack.127), channel_id=1, replica_groups=mesh['seq'=24,'tensor'=32] {'seq'}, use_global_device_ids=true, to_apply=%region_36.0 | all-reduce | flops 1488 | bytes 11904 | tf_op jit(solution)/shard_map/psum | solution.py:96
  390.6 0.6 broadcast_multiply_fusion.2
  391.2 0.7 fusion.135
  391.9 147.4 %all-reduce.3.cloned.1.call-done = (f32[1536,192]{0,1:T(8,128)}, f32[192,1536]{1,0:T(8,128)}) async-done(((f32[1536,192]{0,1:T(8,128)}, f32[192,1536]{1,0:T(8,128)}), (f32[1536,192]{0,1:T(8,128)}, f32[192,1536]{1,0:T(8,128)})) %all-reduce.3.cloned.1.call-update) | async-done | bytes 2359312 | tf_op jit(solution)/shard_map/psum | solution.py:96
  539.3 2.5 broadcast_multiply_fusion.1
  541.8 1.1 broadcast_multiply_fusion
  (123 shorter events, 0.3 us)
Async XLA Ops:
  7.2 7.0 %copy-start = (bf16[192,1536]{1,0:T(8,128)(2,1)S(1)}, bf16[192,1536]{1,0:T(8,128)(2,1)}, u32[]{:S(2)}) copy-start(bf16[192,1536]{1,0:T(8,128)(2,1)} %param.8) | copy-start | bytes 1769476
  7.2 151.4 %reduce-scatter.4.cloned.1.call-start = ((), (), s32[]{:S(2)}) async-start(), calls=%async_computation.2 | async-start | bytes 4866048 | tf_op jit(solution)/shard_map/reduce_scatter | solution.py:45
  23.2 143.5 %copy-start.20 = (s32[2,768]{1,0:T(2,128)S(1)}, s32[2,768]{1,0:T(2,128)}, u32[]{:S(2)}) copy-start(s32[2,768]{1,0:T(2,128)} %param.10) | copy-start | bytes 18436
  23.2 240.3 %all-gather.2.cloned.1.call-start = ((), (), s32[]{:S(2)}) async-start(), calls=%async_computation.1 | async-start | bytes 2433024 | tf_op jit(solution)/shard_map/all_gather | solution.py:78
  159.6 7.5 %collective-permute-start.1 = (bf16[48,15]{1,0:T(8,128)(2,1)S(1)}, bf16[48,15]{1,0:T(8,128)(2,1)S(1)}, u32[]{:S(2)}, u32[]{:S(2)}) collective-permute-start(bf16[48,15]{1,0:T(8,128)(2,1)S(1)} %get-tuple-element.85), channel_id=1, source_target_pairs={{32,0},{64,32},{96,64},{128,96},{160,128},{192,160},{224,192},{256... | collective-permute-start | bytes 4328 | tf_op jit(solution)/shard_map/ppermute | solution.py:19
  160.9 7.2 %collective-permute-start = (bf16[48,15]{1,0:T(8,128)(2,1)S(1)}, bf16[48,15]{1,0:T(8,128)(2,1)S(1)}, u32[]{:S(2)}, u32[]{:S(2)}) collective-permute-start(bf16[48,15]{1,0:T(8,128)(2,1)S(1)} %get-tuple-element.84), channel_id=1, source_target_pairs={{0,32},{32,64},{64,96},{96,128},{128,160},{160,192},{192,224},{224... | collective-permute-start | bytes 4328 | tf_op jit(solution)/shard_map/ppermute | solution.py:16
  167.1 17.5 %copy-start.7 = (f32[768]{0:T(1024)}, f32[768]{0:T(1024)S(1)}, u32[]{:S(2)}) copy-start(f32[768]{0:T(1024)S(1)} %get-tuple-element.121) | copy-start | bytes 9220
  167.1 17.5 %copy-start.9 = (f32[768]{0:T(1024)}, f32[768]{0:T(1024)S(1)}, u32[]{:S(2)}) copy-start(f32[768]{0:T(1024)S(1)} %get-tuple-element.122) | copy-start | bytes 9220
  167.1 17.5 %copy-start.11 = (f32[768]{0:T(1024)}, f32[768]{0:T(1024)S(1)}, u32[]{:S(2)}) copy-start(f32[768]{0:T(1024)S(1)} %get-tuple-element.74) | copy-start | bytes 9220
  167.1 17.5 %copy-start.13 = (f32[768]{0:T(1024)}, f32[768]{0:T(1024)S(1)}, u32[]{:S(2)}) copy-start(f32[768]{0:T(1024)S(1)} %get-tuple-element.125) | copy-start | bytes 9220
  167.1 17.5 %copy-start.15 = (f32[768]{0:T(1024)}, f32[768]{0:T(1024)S(1)}, u32[]{:S(2)}) copy-start(f32[768]{0:T(1024)S(1)} %get-tuple-element.134) | copy-start | bytes 9220
  167.1 17.5 %copy-start.17 = (f32[768]{0:T(1024)}, f32[768]{0:T(1024)S(1)}, u32[]{:S(2)}) copy-start(f32[768]{0:T(1024)S(1)} %get-tuple-element.143) | copy-start | bytes 9220
  168.2 16.4 %copy-start.6 = (bf16[768,48]{0,1:T(8,128)(2,1)S(1)}, bf16[768,48]{0,1:T(8,128)(2,1)}, u32[]{:S(2)}) copy-start(bf16[768,48]{0,1:T(8,128)(2,1)} %param.11) | copy-start | bytes 221188
  168.2 16.4 %copy-start.21 = (f32[48]{0:T(128)S(1)}, f32[48]{0:T(128)}, u32[]{:S(2)}) copy-start(f32[48]{0:T(128)} %get-tuple-element.105) | copy-start | bytes 580
  168.2 16.4 %copy-start.22 = (f32[48]{0:T(128)S(1)}, f32[48]{0:T(128)}, u32[]{:S(2)}) copy-start(f32[48]{0:T(128)} %get-tuple-element.106) | copy-start | bytes 580
  168.2 16.4 %copy-start.23 = (f32[48]{0:T(128)S(1)}, f32[48]{0:T(128)}, u32[]{:S(2)}) copy-start(f32[48]{0:T(128)} %get-tuple-element.107) | copy-start | bytes 580
  168.2 16.4 %copy-start.24 = (f32[48]{0:T(128)S(1)}, f32[48]{0:T(128)}, u32[]{:S(2)}) copy-start(f32[48]{0:T(128)} %get-tuple-element.108) | copy-start | bytes 580
  168.2 16.4 %copy-start.25 = (f32[48]{0:T(128)S(1)}, f32[48]{0:T(128)}, u32[]{:S(2)}) copy-start(f32[48]{0:T(128)} %get-tuple-element.109) | copy-start | bytes 580
  168.2 16.4 %copy-start.26 = (f32[48]{0:T(128)S(1)}, f32[48]{0:T(128)}, u32[]{:S(2)}) copy-start(f32[48]{0:T(128)} %get-tuple-element.110) | copy-start | bytes 580
  168.2 16.4 %copy-start.27 = (f32[48]{0:T(128)S(1)}, f32[48]{0:T(128)}, u32[]{:S(2)}) copy-start(f32[48]{0:T(128)} %get-tuple-element.111) | copy-start | bytes 580
  168.3 16.4 %copy-start.28 = (f32[48]{0:T(128)S(1)}, f32[48]{0:T(128)}, u32[]{:S(2)}) copy-start(f32[48]{0:T(128)} %get-tuple-element.112) | copy-start | bytes 580
  168.3 16.4 %copy-start.29 = (f32[48]{0:T(128)S(1)}, f32[48]{0:T(128)}, u32[]{:S(2)}) copy-start(f32[48]{0:T(128)} %get-tuple-element.113) | copy-start | bytes 580
  168.3 16.4 %copy-start.30 = (f32[48]{0:T(128)S(1)}, f32[48]{0:T(128)}, u32[]{:S(2)}) copy-start(f32[48]{0:T(128)} %get-tuple-element.114) | copy-start | bytes 580
  168.3 16.4 %copy-start.31 = (f32[48]{0:T(128)S(1)}, f32[48]{0:T(128)}, u32[]{:S(2)}) copy-start(f32[48]{0:T(128)} %get-tuple-element.115) | copy-start | bytes 580
  168.3 16.4 %copy-start.32 = (f32[48]{0:T(128)S(1)}, f32[48]{0:T(128)}, u32[]{:S(2)}) copy-start(f32[48]{0:T(128)} %get-tuple-element.116) | copy-start | bytes 580
  168.3 16.4 %copy-start.33 = (f32[48]{0:T(128)S(1)}, f32[48]{0:T(128)}, u32[]{:S(2)}) copy-start(f32[48]{0:T(128)} %get-tuple-element.86) | copy-start | bytes 580
  168.3 16.4 %copy-start.34 = (f32[48]{0:T(128)S(1)}, f32[48]{0:T(128)}, u32[]{:S(2)}) copy-start(f32[48]{0:T(128)} %get-tuple-element.87) | copy-start | bytes 580
  168.3 16.4 %copy-start.35 = (f32[48]{0:T(128)S(1)}, f32[48]{0:T(128)}, u32[]{:S(2)}) copy-start(f32[48]{0:T(128)} %get-tuple-element.88) | copy-start | bytes 580
  168.3 16.4 %copy-start.36 = (f32[48]{0:T(128)S(1)}, f32[48]{0:T(128)}, u32[]{:S(2)}) copy-start(f32[48]{0:T(128)} %get-tuple-element.89) | copy-start | bytes 580
  168.3 16.4 %copy-start.37 = (f32[48]{0:T(128)S(1)}, f32[48]{0:T(128)}, u32[]{:S(2)}) copy-start(f32[48]{0:T(128)} %get-tuple-element.90) | copy-start | bytes 580
  168.4 16.4 %copy-start.38 = (f32[48]{0:T(128)S(1)}, f32[48]{0:T(128)}, u32[]{:S(2)}) copy-start(f32[48]{0:T(128)} %get-tuple-element.91) | copy-start | bytes 580
  168.4 16.4 %copy-start.39 = (f32[48]{0:T(128)S(1)}, f32[48]{0:T(128)}, u32[]{:S(2)}) copy-start(f32[48]{0:T(128)} %get-tuple-element.92) | copy-start | bytes 580
  168.4 16.4 %copy-start.40 = (f32[48]{0:T(128)S(1)}, f32[48]{0:T(128)}, u32[]{:S(2)}) copy-start(f32[48]{0:T(128)} %get-tuple-element.93) | copy-start | bytes 580
  168.4 16.4 %copy-start.41 = (f32[48]{0:T(128)S(1)}, f32[48]{0:T(128)}, u32[]{:S(2)}) copy-start(f32[48]{0:T(128)} %get-tuple-element.94) | copy-start | bytes 580
  168.4 16.4 %copy-start.42 = (f32[48]{0:T(128)S(1)}, f32[48]{0:T(128)}, u32[]{:S(2)}) copy-start(f32[48]{0:T(128)} %get-tuple-element.95) | copy-start | bytes 580
  168.4 16.4 %copy-start.43 = (f32[48]{0:T(128)S(1)}, f32[48]{0:T(128)}, u32[]{:S(2)}) copy-start(f32[48]{0:T(128)} %get-tuple-element.96) | copy-start | bytes 580
  168.4 16.4 %copy-start.44 = (f32[48]{0:T(128)S(1)}, f32[48]{0:T(128)}, u32[]{:S(2)}) copy-start(f32[48]{0:T(128)} %get-tuple-element.97) | copy-start | bytes 580
  168.4 16.4 %copy-start.45 = (f32[48]{0:T(128)S(1)}, f32[48]{0:T(128)}, u32[]{:S(2)}) copy-start(f32[48]{0:T(128)} %get-tuple-element.98) | copy-start | bytes 580
  168.4 16.4 %copy-start.46 = (f32[48]{0:T(128)S(1)}, f32[48]{0:T(128)}, u32[]{:S(2)}) copy-start(f32[48]{0:T(128)} %get-tuple-element.99) | copy-start | bytes 580
  168.4 16.4 %copy-start.47 = (f32[48]{0:T(128)S(1)}, f32[48]{0:T(128)}, u32[]{:S(2)}) copy-start(f32[48]{0:T(128)} %get-tuple-element.100) | copy-start | bytes 580
  168.5 16.4 %copy-start.48 = (f32[48]{0:T(128)S(1)}, f32[48]{0:T(128)}, u32[]{:S(2)}) copy-start(f32[48]{0:T(128)} %get-tuple-element.101) | copy-start | bytes 580
  168.5 16.4 %copy-start.49 = (f32[48]{0:T(128)S(1)}, f32[48]{0:T(128)}, u32[]{:S(2)}) copy-start(f32[48]{0:T(128)} %get-tuple-element.102) | copy-start | bytes 580
  168.5 16.4 %copy-start.50 = (f32[48]{0:T(128)S(1)}, f32[48]{0:T(128)}, u32[]{:S(2)}) copy-start(f32[48]{0:T(128)} %get-tuple-element.103) | copy-start | bytes 580
  168.5 16.4 %copy-start.51 = (f32[48]{0:T(128)S(1)}, f32[48]{0:T(128)}, u32[]{:S(2)}) copy-start(f32[48]{0:T(128)} %get-tuple-element.104) | copy-start | bytes 580
  168.5 95.0 %copy-start.3 = (bf16[768,1536]{1,0:T(8,128)(2,1)S(1)}, bf16[768,1536]{1,0:T(8,128)(2,1)}, u32[]{:S(2)}) copy-start(bf16[768,1536]{1,0:T(8,128)(2,1)} %copy-done.2) | copy-start | bytes 7077892
  172.2 6.9 %collective-permute-start.3 = (f32[48,15]{1,0:T(8,128)S(1)}, f32[48,15]{1,0:T(8,128)S(1)}, u32[]{:S(2)}, u32[]{:S(2)}) collective-permute-start(f32[48,15]{1,0:T(8,128)S(1)} %get-tuple-element.83), channel_id=1, source_target_pairs={{0,32},{32,64},{64,96},{96,128},{128,160},{160,192},{192,224},{224... | collective-permute-start | bytes 8648 | tf_op jit(solution)/shard_map/ppermute | solution.py:16
  177.6 6.9 %collective-permute-start.2 = (f32[48,15]{1,0:T(8,128)S(1)}, f32[48,15]{1,0:T(8,128)S(1)}, u32[]{:S(2)}, u32[]{:S(2)}) collective-permute-start(f32[48,15]{1,0:T(8,128)S(1)} %get-tuple-element.82), channel_id=1, source_target_pairs={{32,0},{64,32},{96,64},{128,96},{160,128},{192,160},{224,192},{256... | collective-permute-start | bytes 8648 | tf_op jit(solution)/shard_map/ppermute | solution.py:19
  187.4 351.9 %all-reduce.3.cloned.1.call-start = ((), (), s32[]{:S(2)}) async-start(), calls=%async_computation.3 | async-start | bytes 4718592 | tf_op jit(solution)/shard_map/psum | solution.py:96
  (21 other events, 30.6 us)
Sparse Core Ops, SparseCore 0:
  23.3 135.2 reduce-scatter.3
  187.5 75.9 all-gather.1
  271.7 267.5 all-reduce.2
where the time goes:
time: 550 us; the launch traced here: 549 us
  waiting for transfers between devices  363 us (66%)
  blocking collectives  116 us (21%)
  other arithmetic  17.6 us (3%)
  between operations  14.7 us (3%)
  starting transfers between devices  14 us (3%)
  matrix products  11.9 us (2%)
  local copies, waits for them, and re-layouts  11.4 us (2%)
    psum x1, waiting for transfers between devices, body(): lax.psum((grad_up, grad_down, grad_kernel), 'seq')  147 us
    reduce_scatter x1, waiting for transfers between devices, body(): lax.psum_scatter(0.5 * lax.dot_general(block, hidden, (((0,), (1,)), ((),...  133 us
    psum x1, blocking collectives, body(): lax.psum((grad_up, grad_down, grad_kernel), 'seq')  116 us
    all_gather x1, waiting for transfers between devices, body(): piece = lax.all_gather(grad_mixed, 'tensor', axis=0, tiled=True)  75.9 us
    ppermute x2, starting transfers between devices, extended(): lax.ppermute(lax.slice_in_dim(block, block.shape[dim] - width, None, axis...  11.2 us
  transfers between devices with their start and end apart: 7, of which 6 were waited for; matrix products, arithmetic and copies ran while one was open for 1% of the time, Pallas kernels for 0%

commit v1 on v0

v1 whole, which is shorter than its diff:
```python
import math

import jax
import jax.numpy as jnp
from jax import lax
from jax.experimental import pallas as pl
from jax.experimental.pallas import tpu as pltpu
from jax.sharding import PartitionSpec as P

MESH = pl.DeviceIdType.MESH
K = 31
HALF = K // 2
NY, NW, NZ, NX = 8, 3, 4, 4
LANES = 128
WAYS = ((1, 3), (3, 1))
HOPS = ((4, 3), (3, 4))
COPIES = 109
F32, BF16 = jnp.float32, jnp.bfloat16


def flip(index, mask):
    if mask == 0:
        return index
    if mask == 1:
        return index + 1 - 2 * lax.rem(index, 2)
    if mask == 2:
        return lax.rem(index + 2, 4)
    return 3 - index


def relative(place, way):
    first, second = WAYS[way]
    return (first if place & 1 else 0) ^ (second if place & 2 else 0)


def dot(a, b, a_dim, b_dim):
    return lax.dot_general(a, b, (((a_dim,), (b_dim,)), ((), ())), preferred_element_type=F32)


def kernel(
    frames,
    w_up,
    w_down,
    taps,
    bounds,
    cot,
    out_t,
    kernel_sum,
    grads,
    normed,
    w_up_t,
    w_down_t,
    ordered,
    act,
    sig,
    hidden,
    keep,
    rs_send,
    rs_recv,
    own,
    x_ext,
    cot_ext,
    edge_send,
    edge_recv,
    cot_send,
    cot_recv,
    masks,
    tap_box,
    gathered,
    piece,
    grad_act,
    totals,
    ring_send,
    ring_recv,
    cross_send,
    cross_recv,
    whole,
    kernel_ring,
    kernel_cross,
    send_sems,
    recv_sems,
):
    length, depth = frames.shape
    width = taps.shape[1]
    hid = w_up.shape[1]
    ext = length + 2 * LANES
    seq, ten = lax.axis_index("seq"), lax.axis_index("tensor")
    y, w = lax.div(seq, NW), lax.rem(seq, NW)
    core, x, z = lax.rem(ten, 2), lax.rem(lax.div(ten, 2), NX), lax.div(ten, 2 * NX)

    def tensor_at(z, x, core):
        return (z * NX + x) * 2 + core

    def x_way(mask):
        return (seq, tensor_at(z, flip(x, mask), core))

    def z_way(mask):
        return (seq, tensor_at(flip(z, mask), x, core))

    def y_way(step):
        return (lax.rem(y + NY + step, NY) * NW + w, ten)

    def w_way(step):
        return (y * NW + lax.rem(w + step, NW), ten)

    sibling = (seq, tensor_at(z, x, 1 - core))
    count = NY * NW
    after = (lax.rem(seq + 1, count), ten)
    before = (lax.rem(seq + count - 1, count), ten)

    barrier = pltpu.get_barrier_semaphore()
    partners = [sibling, x_way(1), x_way(3), z_way(1), z_way(3), after, before]
    partners += [y_way(1), y_way(-1), w_way(1), w_way(2)]
    for partner in partners:
        pl.semaphore_signal(barrier, inc=1, device_id=partner, device_id_type=MESH)

    started = []

    def send(src, dst, target):
        spot = len(started)
        copy = pltpu.make_async_remote_copy(
            src_ref=src,
            dst_ref=dst,
            send_sem=send_sems.at[spot],
            recv_sem=recv_sems.at[spot],
            device_id=target,
            device_id_type=MESH,
        )
        copy.start()
        started.append(copy)
        return copy

    block = LANES

    def normalise(i, carry):
        rows = pl.ds(pl.multiple_of(i * block, block), block)
        wide = frames[rows, :].astype(F32)
        mean = jnp.mean(wide, axis=1, keepdims=True)
        centred = wide - mean
        var = jnp.mean(centred * centred, axis=1, keepdims=True)
        normed[rows, :] = (centred / jnp.sqrt(var + 1e-05)).astype(BF16)
        return carry

    lax.fori_loop(0, length // block, normalise, 0)
    w_up_t[...] = w_up[...].astype(F32).T.astype(BF16)
    w_down_t[...] = w_down[...].astype(F32).T.astype(BF16)
    for way in range(2):
        for c in range(2):
            for i in range(NX):
                for j in range(NZ):
                    home = tensor_at(
                        flip(z, relative(j, way)),
                        flip(x, relative(i, way)),
                        1 - core if c else core,
                    )
                    spot = (c * NX + i) * NZ + j
                    ordered[way, spot * width : (spot + 1) * width, :] = w_down_t[
                        pl.ds(pl.multiple_of(home * width, 16), width), :
                    ]
    up = dot(w_up_t[...], normed[...], 1, 1)
    gate = jax.nn.sigmoid(up)
    act[...] = up
    sig[...] = gate
    hidden[...] = (up * gate).astype(BF16)
    cot_t = dot(
        (
            lax.broadcasted_iota(jnp.int32, (width, width), 0)
            == lax.broadcasted_iota(jnp.int32, (width, width), 1)
        ).astype(BF16),
        cot[...],
        1,
        1,
    )
    cot_ext[:, LANES : LANES + length] = cot_t
    cot_send[0] = cot_t[:, length - LANES :].astype(BF16)
    cot_send[1] = cot_t[:, :LANES].astype(BF16)

    pl.semaphore_wait(barrier, len(partners))

    half = depth // 2
    starts, height = [], half
    offset = 0
    for _ in range(5):
        starts.append((offset, height))
        offset += height
        height //= 2
    chunks = length // LANES
    units = [((i, 0), (chunks - 1 - i, 1)) for i in range(chunks // 2)]

    def rs_start(stage, chunk, way):
        first, second = WAYS[way]
        target = (sibling, x_way(second), x_way(first), z_way(second), z_way(first))[stage]
        low, rows = starts[stage]
        return send(
            rs_send.at[chunk, pl.ds(low, rows), :], rs_recv.at[chunk, pl.ds(low, rows), :], target
        )

    flights = {}
    for unit in units:
        for chunk, way in unit:
            columns = slice(chunk * LANES, (chunk + 1) * LANES)
            part = hidden[:, columns]
            rs_send[chunk, 0:half, :] = dot(ordered[way, half:, :], part, 1, 0).astype(BF16)
            flights[0, chunk] = rs_start(0, chunk, way)
        for chunk, way in unit:
            columns = slice(chunk * LANES, (chunk + 1) * LANES)
            keep[chunk] = dot(ordered[way, :half, :], hidden[:, columns], 1, 0)

    cot_copies = [
        send(cot_send.at[0], cot_recv.at[0], after),
        send(cot_send.at[1], cot_recv.at[1], before),
    ]

    pick = (
        lax.broadcasted_iota(jnp.int32, (width, depth), 1)
        == ten * width + lax.broadcasted_iota(jnp.int32, (width, depth), 0)
    ).astype(BF16)
    own[...] = dot(pick, frames[...], 1, 1)
    limits = bounds[...]
    limits = jnp.concatenate(
        [
            jnp.broadcast_to(limits[:, :1], (2, LANES)),
            limits,
            jnp.broadcast_to(limits[:, length - 1 :], (2, LANES)),
        ],
        axis=1,
    )
    lower = jnp.broadcast_to(limits[0:1, :], (8, ext))
    upper = jnp.broadcast_to(limits[1:2, :], (8, ext))
    spots = seq * length - LANES + lax.broadcasted_iota(jnp.int32, (8, ext), 1)
    for tap in range(K):
        target = spots + (tap - HALF)
        masks[tap] = jnp.where((target >= lower) & (target < upper), 1.0, 0.0).astype(F32)
    tap_box[...] = jnp.zeros((LANES, LANES), F32)
    tap_box[0:K, 0:width] = taps[...]
    tap_box[...] = tap_box[...].T

    edges = {}

    def rs_finish(stage, chunk, way):
        flights[stage, chunk].wait_recv()
        low, rows = starts[stage]
        if stage < 4:
            mid = rows // 2
            nxt = starts[stage + 1][0]
            rs_send[chunk, nxt : nxt + mid, :] = (
                keep[chunk, mid:rows, :] + rs_recv[chunk, low + mid : low + rows, :].astype(F32)
            ).astype(BF16)
            flights[stage + 1, chunk] = rs_start(stage + 1, chunk, way)
            keep[chunk, 0:mid, :] = keep[chunk, 0:mid, :] + rs_recv[
                chunk, low : low + mid, :
            ].astype(F32)
            return
        columns = slice(chunk * LANES, (chunk + 1) * LANES)
        branch = keep[chunk, 0:rows, :] + rs_recv[chunk, low : low + rows, :].astype(F32)
        mixed = (own[:, columns] + 0.5 * branch).astype(BF16)
        x_ext[:, (chunk + 1) * LANES : (chunk + 2) * LANES] = mixed.astype(F32)
        if chunk == 0:
            edge_send[1] = mixed
            edges[1] = send(edge_send.at[1], edge_recv.at[1], before)
        if chunk == chunks - 1:
            edge_send[0] = mixed
            edges[0] = send(edge_send.at[0], edge_recv.at[0], after)

    for turn in range(len(units) + 4):
        for stage in range(5):
            if 0 <= turn - stage < len(units):
                for chunk, way in units[turn - stage]:
                    rs_finish(stage, chunk, way)

    for side, low in ((0, 0), (1, ext - LANES)):
        cot_copies[side].wait_recv()
        cot_ext[:, low : low + LANES] = cot_recv[side].astype(F32)
    for side, low in ((0, 0), (1, ext - LANES)):
        edges[side].wait_recv()
        x_ext[:, low : low + LANES] = edge_recv[side].astype(F32)

    lane = lax.broadcasted_iota(jnp.int32, (8, LANES), 1)
    groups = width // 16
    columns_of = (slice(0, length // 2), slice(length // 2, length))
    inner = slice(LANES, LANES + length)

    def convolve(group):
        rows = pl.ds(pl.multiple_of(group * 8, 8), 8)
        here = x_ext[rows, :]
        cot_here = cot_ext[rows, :]
        tap_here = tap_box[rows, :]
        conv = jnp.zeros((8, ext), F32)
        for tap in range(K):
            moved = pltpu.roll(here, (HALF - tap) % ext, 1) if tap != HALF else here
            conv = conv + tap_here[:, tap : tap + 1] * (moved * masks[tap])
        conv_sig = jax.nn.sigmoid(conv)
        grad = cot_here * conv_sig * (1.0 + conv * (1.0 - conv_sig))
        out_t[rows, :] = (here + conv * conv_sig)[:, inner]
        total = cot_here
        sums = jnp.zeros((8, LANES), F32)
        here = here[:, inner]
        for tap in range(K):
            moved = pltpu.roll(grad, (tap - HALF) % ext, 1) if tap != HALF else grad
            moved = moved * masks[K - 1 - tap]
            total = total + tap_here[:, tap : tap + 1] * moved
            term = jnp.sum(moved[:, inner] * here, axis=1, keepdims=True)
            sums = jnp.where(lane == tap, term, sums)
        kernel_ring[y, rows, :] = sums
        return total[:, inner]

    ag = {}

    def ag_start(stage, unit, way):
        first, second = WAYS[way]
        target = (z_way(first), z_way(second), x_way(first), x_way(second), sibling)[stage]
        rows = 16 << stage
        return send(
            gathered.at[unit, way, pl.ds(0, rows), :],
            gathered.at[unit, way, pl.ds(rows, rows), :],
            target,
        )

    for unit in range(groups):
        grad_mixed = jnp.concatenate([convolve(2 * unit), convolve(2 * unit + 1)], axis=0)
        for way in range(2):
            gathered[unit, way, 0:16, :] = grad_mixed[:, columns_of[way]].astype(BF16)
            ag[0, unit, way] = ag_start(0, unit, way)

    taps_flight = {}

    def taps_start(hop):
        for step, hops in ((1, 4), (-1, 3)):
            if hop > hops:
                continue
            spot = lax.rem(y + NY - step * (hop - 1), NY)
            taps_flight[hop, step] = send(kernel_ring.at[spot], kernel_ring.at[spot], y_way(step))

    def taps_wait(hop):
        for step in (1, -1):
            if (hop, step) in taps_flight:
                taps_flight[hop, step].wait_recv()

    taps_start(1)

    def ag_finish(stage, unit):
        for way in range(2):
            ag[stage, unit, way].wait_recv()
            if stage < 4:
                ag[stage + 1, unit, way] = ag_start(stage + 1, unit, way)
                continue
            for c in range(2):
                for i in range(NX):
                    for j in range(NZ):
                        home = tensor_at(
                            flip(z, relative(j, way)),
                            flip(x, relative(i, way)),
                            1 - core if c else core,
                        )
                        spot = (c * NX + i) * NZ + j
                        piece[
                            pl.ds(pl.multiple_of(home * width + 16 * unit, 16), 16),
                            columns_of[way],
                        ] = gathered[unit, way, spot * 16 : (spot + 1) * 16, :]

    for turn in range(groups + 4):
        for stage in range(5):
            if 0 <= turn - stage < groups:
                ag_finish(stage, turn - stage)
        if turn in (1, 2, 3):
            taps_wait(turn)
            taps_start(turn + 1)
    taps_wait(4)
    total = kernel_ring[0]
    for i in range(1, NY):
        total = total + kernel_ring[i]
    kernel_cross[w] = total
    cross = [send(kernel_cross.at[w], kernel_cross.at[w], w_way(step)) for step in (1, 2)]

    tall, broad = hid // 2, depth // 4

    def down_chunk(d):
        low, left = tall * (d % 2), broad * (d // 2)
        totals[0, d] = dot(hidden[low : low + tall, :], piece[left : left + broad, :], 1, 1)

    def up_chunk(d):
        low, left = tall * (d % 2), broad * (d // 2)
        totals[1, d] = dot(grad_act[low : low + tall, :], normed[:, left : left + broad], 1, 0)

    ring = {}

    def ring_spot(stream, side, k):
        return (stream * 2 + side) * 4 + k - 1

    def ring_start(stream, side, k):
        step = (1, -1)[side]
        if k > HOPS[stream][side]:
            return
        chunk = lax.rem(y + NY + step * k, NY)
        value = totals[stream, chunk]
        if k < HOPS[stream][side]:
            ring[stream, side, k + 1].wait_recv()
            value = value + ring_recv[ring_spot(stream, side, k + 1)].astype(F32)
        spot = ring_spot(stream, side, k)
        ring_send[spot] = value.astype(BF16)
        ring[stream, side, k] = send(ring_send.at[spot], ring_recv.at[spot], y_way(step))

    for d in range(8):
        down_chunk(d)
    ring_start(0, 0, 4)
    ring_start(0, 1, 3)
    grad_hidden = 0.5 * dot(w_down[...], piece[...], 1, 0)
    gate = sig[...]
    grad_act[...] = (grad_hidden * gate * (1.0 + act[...] * (1.0 - gate))).astype(BF16)
    for d in range(8):
        up_chunk(d)
    ring_start(1, 1, 4)
    ring_start(1, 0, 3)
    ring_start(0, 0, 3)
    ring_start(1, 1, 3)
    for k in (2, 1):
        ring_start(0, 1, k)
        ring_start(1, 0, k)
        ring_start(0, 0, k)
        ring_start(1, 1, k)

    third = tall // NW
    cross_flight = {}
    for stream in range(2):
        for side in range(2):
            ring[stream, side, 1].wait_recv()
        totals[stream, y] = (
            totals[stream, y]
            + ring_recv[ring_spot(stream, 0, 1)].astype(F32)
            + ring_recv[ring_spot(stream, 1, 1)].astype(F32)
        )
        for step in (1, 2):
            rows = pl.ds(pl.multiple_of(lax.rem(w + step, NW) * third, third), third)
            cross_send[stream * 2 + step - 1] = totals[stream, y, rows, :].astype(BF16)
            cross_flight[stream, step] = send(
                cross_send.at[stream * 2 + step - 1],
                cross_recv.at[stream * 2 + step - 1],
                w_way(step),
            )
    for copy in cross:
        copy.wait_recv()
    kernel_sum[...] = kernel_cross[0] + kernel_cross[1] + kernel_cross[2]
    mine = pl.ds(pl.multiple_of(w * third, third), third)
    share = {}
    for stream in range(2):
        value = totals[stream, y, mine, :]
        for step in (1, 2):
            cross_flight[stream, step].wait_recv()
            value = value + cross_recv[stream * 2 + step - 1].astype(F32)
        whole[stream, y, mine, :] = value.astype(BF16)
        for step in (1, 2):
            share[stream, step] = send(
                whole.at[stream, y, mine, :], whole.at[stream, y, mine, :], w_way(step)
            )
    spread = {}
    for k in range(1, 6):
        for stream in range(2):
            if k == 1:
                for step in (1, 2):
                    share[stream, step].wait_recv()
            for side in range(2):
                step = (1, -1)[side]
                if 1 < k <= HOPS[stream][side] + 1:
                    spread[stream, side, k - 1].wait_recv()
                if k <= HOPS[stream][side]:
                    spot = lax.rem(y + NY - step * (k - 1), NY)
                    spread[stream, side, k] = send(
                        whole.at[stream, spot], whole.at[stream, spot], y_way(step)
                    )
    grads[...] = whole[...]
    for copy in started:
        copy.wait_send()


def body(frames, w_up, w_down, taps, bounds, cot):
    length, depth = frames.shape
    width = taps.shape[1]
    hid = w_up.shape[1]
    ext = length + 2 * LANES
    chunks = length // LANES
    rs_rows = depth // 2 + depth // 4 + depth // 8 + depth // 16 + depth // 32
    block = (hid // 2, depth // 4)
    vmem = pl.BlockSpec(memory_space=pltpu.VMEM)
    out_t, kernel_sum, grads = pl.pallas_call(
        kernel,
        out_shape=(
            jax.ShapeDtypeStruct((width, length), F32),
            jax.ShapeDtypeStruct((width, LANES), F32),
            jax.ShapeDtypeStruct((2, NY, *block), BF16),
        ),
        in_specs=[vmem] * 6,
        out_specs=(vmem,) * 3,
        scratch_shapes=[
            pltpu.VMEM((length, depth), BF16),
            pltpu.VMEM((hid, depth), BF16),
            pltpu.VMEM((depth, hid), BF16),
            pltpu.VMEM((2, depth, hid), BF16),
            pltpu.VMEM((hid, length), F32),
            pltpu.VMEM((hid, length), F32),
            pltpu.VMEM((hid, length), BF16),
            pltpu.VMEM((chunks, depth // 2, LANES), F32),
            pltpu.VMEM((chunks, rs_rows, LANES), BF16),
            pltpu.VMEM((chunks, rs_rows, LANES), BF16),
            pltpu.VMEM((width, length), F32),
            pltpu.VMEM((width, ext), F32),
            pltpu.VMEM((width, ext), F32),
            pltpu.VMEM((2, width, LANES), BF16),
            pltpu.VMEM((2, width, LANES), BF16),
            pltpu.VMEM((2, width, LANES), BF16),
            pltpu.VMEM((2, width, LANES), BF16),
            pltpu.VMEM((K, 8, ext), F32),
            pltpu.VMEM((LANES, LANES), F32),
            pltpu.VMEM((width // 16, 2, depth // width * 16, length // 2), BF16),
            pltpu.VMEM((depth, length), BF16),
            pltpu.VMEM((hid, length), BF16),
            pltpu.VMEM((2, NY, *block), F32),
            pltpu.VMEM((16, *block), BF16),
            pltpu.VMEM((16, *block), BF16),
            pltpu.VMEM((4, block[0] // NW, block[1]), BF16),
            pltpu.VMEM((4, block[0] // NW, block[1]), BF16),
            pltpu.VMEM((2, NY, *block), BF16),
            pltpu.VMEM((NY, width, LANES), F32),
            pltpu.VMEM((NW, width, LANES), F32),
            pltpu.SemaphoreType.DMA((COPIES,)),
            pltpu.SemaphoreType.DMA((COPIES,)),
        ],
        compiler_params=pltpu.CompilerParams(
            collective_id=0, has_side_effects=True, vmem_limit_bytes=60 << 20
        ),
    )(frames, w_up, w_down, taps, bounds, cot)
    scale = 1.0 / math.sqrt(length * NY * NW)
    down, up = (
        part.reshape(4, 2, *block).transpose(1, 2, 0, 3).reshape(hid, depth).astype(F32)
        for part in (grads[0], grads[1])
    )
    output = out_t.astype(BF16).T
    return output, up.T * scale, down * (0.5 * scale), kernel_sum[:, :K].T * scale


def solution(mesh):
    return jax.shard_map(
        body,
        mesh=mesh,
        in_specs=(
            P("seq", None),
            P(None, "tensor"),
            P("tensor", None),
            P(None, "tensor"),
            P(None, "seq"),
            P("seq", "tensor"),
        ),
        out_specs=(P("seq", "tensor"), P(None, "tensor"), P("tensor", None), P(None, "tensor")),
        check_vma=False,
    )
```

time: 550 us -> 136 us (0.25)
  the two profiles are of different devices: /device:TPU:196 before, /device:TPU:2 now
where the time goes in v1:
time: 136 us
  Pallas kernels  123 us (90%)
  local copies, waits for them, and re-layouts  8.31 us (6%)
  other arithmetic  3.81 us (3%)
    pallas_call x1, Pallas kernels, body(): pl.pallas_call(kernel, out_shape=(jax.ShapeDtypeStruct((width, length), F...  123 us
    unnamed x5, local copies, waits for them, and re-layouts  6.79 us

profile of v1, /device:TPU:2, one launch (start us, length us, event | category | flops | bytes accessed | tf_op | source)
XLA Modules:
  0.0 135.9 jit_solution(1075818012720823420)
XLA Ops:
  0.6 1.7 %copy.11.cot = bf16[768,48]{1,0:T(8,128)(2,1)} copy(bf16[768,48]{0,1:T(8,128)(2,1)} %param.11) | data formatting | bytes 147456 | tf_op args[5]
  2.3 2.2 %copy.10.w_up = bf16[1536,192]{1,0:T(8,128)(2,1)} copy(bf16[1536,192]{0,1:T(8,128)(2,1)} %param.7) | data formatting | bytes 1179648 | tf_op args[1]
  4.5 123.1 %shard_map.93 = (f32[48,768]{1,0:T(8,128)}, f32[48,128]{1,0:T(8,128)}, bf16[2,8,96,384]{3,2,1,0:T(8,128)(2,1)}) custom-call(bf16[768,1536]{1,0:T(8,128)(2,1)} %frames.1, bf16[1536,192]{1,0:T(8,128)(2,1)} %copy.10.w_up, bf16[192,1536]{1,0:T(8,128)(2,1)} %w_down.1, f32[31,48]{1,0:T(8,128)} %taps.1, s32[2,768]{1,0:T(2,128)} %bounds.1, bf16[768,48]{1,0:T(8,128)(2,1)} %copy.11.cot), custom_call_target="tpu_custom_call" | custom-call | tf_op jit(solution)/shard_map/pallas_call | solution.py:484
  127.7 1.6 %convert_bitcast_fusion = bf16[768,48]{0,1:T(8,128)(2,1)} fusion(f32[48,768]{1,0:T(8,128)} %get-tuple-element.7), kind=kLoop, calls=%fused_computation.2 | loop fusion | flops 36864 | bytes 221184 | tf_op jit(solution)/shard_map/transpose | solution.py:536
  129.2 0.7 multiply_bitcast_fusion
  130.0 0.7 copy.14
  130.7 1.5 %convert_multiply_fusion = (f32[1,8,96,384]{3,2,1,0:T(8,128)S(1)}, f32[1,8,96,384]{3,2,1,0:T(8,128)S(1)}) fusion(bf16[2,8,96,384]{3,2,1,0:T(8,128)(2,1)} %get-tuple-element.8), kind=kLoop, calls=%fused_computation | loop fusion | flops 1179648 | bytes 3538944 | tf_op jit(solution)/shard_map/mul | solution.py:537
  132.2 0.8 copy.13
  133.0 1.1 copy.16
  134.0 0.8 copy.12
  134.8 1.1 copy.15

commit v2 on v1

--- a/solution.py
+++ b/solution.py
@@ -39,16 +39,15 @@
 
 def kernel(
     frames,
-    w_up,
+    w_up_t,
     w_down,
     taps,
     bounds,
-    cot,
+    cot_t,
     out_t,
     kernel_sum,
     grads,
     normed,
-    w_up_t,
     w_down_t,
     ordered,
     act,
@@ -82,7 +81,7 @@
 ):
     length, depth = frames.shape
     width = taps.shape[1]
-    hid = w_up.shape[1]
+    hid = w_up_t.shape[0]
     ext = length + 2 * LANES
     seq, ten = lax.axis_index("seq"), lax.axis_index("tensor")
     y, w = lax.div(seq, NW), lax.rem(seq, NW)
@@ -142,7 +141,6 @@
         return carry
 
     lax.fori_loop(0, length // block, normalise, 0)
-    w_up_t[...] = w_up[...].astype(F32).T.astype(BF16)
     w_down_t[...] = w_down[...].astype(F32).T.astype(BF16)
     for way in range(2):
         for c in range(2):
@@ -162,18 +160,9 @@
     act[...] = up
     sig[...] = gate
     hidden[...] = (up * gate).astype(BF16)
-    cot_t = dot(
-        (
-            lax.broadcasted_iota(jnp.int32, (width, width), 0)
-            == lax.broadcasted_iota(jnp.int32, (width, width), 1)
-        ).astype(BF16),
-        cot[...],
-        1,
-        1,
-    )
-    cot_ext[:, LANES : LANES + length] = cot_t
-    cot_send[0] = cot_t[:, length - LANES :].astype(BF16)
-    cot_send[1] = cot_t[:, :LANES].astype(BF16)
+    cot_ext[:, LANES : LANES + length] = cot_t[...].astype(F32)
+    cot_send[0] = cot_t[:, length - LANES :]
+    cot_send[1] = cot_t[:, :LANES]
 
     pl.semaphore_wait(barrier, len(partners))
 
@@ -291,7 +280,7 @@
             conv = conv + tap_here[:, tap : tap + 1] * (moved * masks[tap])
         conv_sig = jax.nn.sigmoid(conv)
         grad = cot_here * conv_sig * (1.0 + conv * (1.0 - conv_sig))
-        out_t[rows, :] = (here + conv * conv_sig)[:, inner]
+        output = (here + conv * conv_sig)[:, inner]
         total = cot_here
         sums = jnp.zeros((8, LANES), F32)
         here = here[:, inner]
@@ -302,7 +291,7 @@
             term = jnp.sum(moved[:, inner] * here, axis=1, keepdims=True)
             sums = jnp.where(lane == tap, term, sums)
         kernel_ring[y, rows, :] = sums
-        return total[:, inner]
+        return output, total[:, inner]
 
     ag = {}
 
@@ -317,7 +306,9 @@
         )
 
     for unit in range(groups):
-        grad_mixed = jnp.concatenate([convolve(2 * unit), convolve(2 * unit + 1)], axis=0)
+        parts = [convolve(2 * unit), convolve(2 * unit + 1)]
+        output, grad_mixed = (jnp.concatenate(pair, axis=0) for pair in zip(*parts))
+        out_t[16 * unit : 16 * unit + 16, :] = output.astype(BF16)
         for way in range(2):
             gathered[unit, way, 0:16, :] = grad_mixed[:, columns_of[way]].astype(BF16)
             ag[0, unit, way] = ag_start(0, unit, way)
@@ -439,7 +430,9 @@
             )
     for copy in cross:
         copy.wait_recv()
-    kernel_sum[...] = kernel_cross[0] + kernel_cross[1] + kernel_cross[2]
+    scale = 1.0 / math.sqrt(length * count)
+    tap_box[0:width, :] = (kernel_cross[0] + kernel_cross[1] + kernel_cross[2]) * scale
+    kernel_sum[...] = tap_box[...].T[0:K, 0:width]
     mine = pl.ds(pl.multiple_of(w * third, third), third)
     share = {}
     for stream in range(2):
@@ -467,7 +460,10 @@
                     spread[stream, side, k] = send(
                         whole.at[stream, spot], whole.at[stream, spot], y_way(step)
                     )
-    grads[...] = whole[...]
+    for stream in range(2):
+        for d in range(8):
+            low, left = tall * (d % 2), broad * (d // 2)
+            grads[stream, low : low + tall, left : left + broad] = whole[stream, d]
     for copy in started:
         copy.wait_send()
 
@@ -484,15 +480,14 @@
     out_t, kernel_sum, grads = pl.pallas_call(
         kernel,
         out_shape=(
-            jax.ShapeDtypeStruct((width, length), F32),
-            jax.ShapeDtypeStruct((width, LANES), F32),
-            jax.ShapeDtypeStruct((2, NY, *block), BF16),
+            jax.ShapeDtypeStruct((width, length), BF16),
+            jax.ShapeDtypeStruct((K, width), F32),
+            jax.ShapeDtypeStruct((2, hid, depth), BF16),
         ),
         in_specs=[vmem] * 6,
         out_specs=(vmem,) * 3,
         scratch_shapes=[
             pltpu.VMEM((length, depth), BF16),
-            pltpu.VMEM((hid, depth), BF16),
             pltpu.VMEM((depth, hid), BF16),
             pltpu.VMEM((2, depth, hid), BF16),
             pltpu.VMEM((hid, length), F32),
@@ -527,14 +522,10 @@
         compiler_params=pltpu.CompilerParams(
             collective_id=0, has_side_effects=True, vmem_limit_bytes=60 << 20
         ),
-    )(frames, w_up, w_down, taps, bounds, cot)
+    )(frames, w_up.T, w_down, taps, bounds, cot.T)
     scale = 1.0 / math.sqrt(length * NY * NW)
-    down, up = (
-        part.reshape(4, 2, *block).transpose(1, 2, 0, 3).reshape(hid, depth).astype(F32)
-        for part in (grads[0], grads[1])
-    )
-    output = out_t.astype(BF16).T
-    return output, up.T * scale, down * (0.5 * scale), kernel_sum[:, :K].T * scale
+    down, up = grads[0].astype(F32) * (0.5 * scale), grads[1].astype(F32) * scale
+    return out_t.T, up.T, down, kernel_sum
 
 
 def solution(mesh):

time: 136 us -> 128 us (0.941)
  local copies, waits for them, and re-layouts: 8.31 us -> 1.25 us
    unnamed x5 -> x6, local copies, waits for them, and re-layouts: 6.79 us -> 1.25 us
    transpose x1 -> x0, other arithmetic: 1.55 us -> none  [body(): output = out_t.astype(BF16).T]
    mul x2 -> x0, local copies, waits for them, and re-layouts: 1.52 us -> none  [the longest x1 0.76 us: body(): down * (0.5 * scale)]
    mul x2 -> x1, other arithmetic: 2.26 us -> 2.98 us  [body(): grads[0].astype(F32) * (0.5 * scale)]
where the time goes in v2:
time: 128 us
  Pallas kernels  123 us (96%)
  other arithmetic  2.98 us (2%)
    pallas_call x1, Pallas kernels, body(): pl.pallas_call(kernel, out_shape=(jax.ShapeDtypeStruct((width, length), B...  123 us
    mul x1, other arithmetic, body(): grads[0].astype(F32) * (0.5 * scale)  2.98 us

profile of v2, /device:TPU:2, one launch (start us, length us, event | category | flops | bytes accessed | tf_op | source)
XLA Modules:
  0.0 127.6 jit_solution(16097897458452463928)
XLA Ops:
  0.6 122.8 %shard_map.93 = (bf16[48,768]{1,0:T(8,128)(2,1)}, f32[31,48]{1,0:T(8,128)}, bf16[2,192,1536]{2,1,0:T(8,128)(2,1)}) custom-call(bf16[768,1536]{1,0:T(8,128)(2,1)} %frames.1, bf16[192,1536]{1,0:T(8,128)(2,1)} %bitcast.9, bf16[192,1536]{1,0:T(8,128)(2,1)} %w_down.1, f32[31,48]{1,0:T(8,128)} %taps.1, s32[2,768]{1,0:T(2,128)} %bounds.1, bf16[48,768]{1,0:T(8,128)(2,1)} %bitcast.11), custom_call_target="tpu_custom_call" | custom-call | tf_op jit(solution)/shard_map/pallas_call | solution.py:480
  123.4 0.0 copy-start
  123.4 0.0 copy-start.1
  123.4 3.0 %multiply_bitcast_fusion = (f32[192,1536]{1,0:T(8,128)}, f32[1536,192]{0,1:T(8,128)}) fusion(bf16[2,192,1536]{2,1,0:T(8,128)(2,1)} %get-tuple-element.8), kind=kLoop, calls=%fused_computation | loop fusion | flops 1179648 | bytes 3538944 | tf_op jit(solution)/shard_map/mul | solution.py:527
  126.4 0.0 copy-done
  126.4 0.6 copy.12
  127.0 0.0 copy-done.1
  127.0 0.6 copy.13
Async XLA Ops:
  123.4 3.0 %copy-start = (bf16[48,768]{1,0:T(8,128)(2,1)S(1)}, bf16[48,768]{1,0:T(8,128)(2,1)}, u32[]{:S(2)}) copy-start(bf16[48,768]{1,0:T(8,128)(2,1)} %get-tuple-element.7) | copy-start | bytes 221188
  123.4 3.6 %copy-start.1 = (f32[31,48]{1,0:T(8,128)S(1)}, f32[31,48]{1,0:T(8,128)}, u32[]{:S(2)}) copy-start(f32[31,48]{1,0:T(8,128)} %get-tuple-element.19) | copy-start | bytes 17860

commit v3 on v2

--- a/solution.py
+++ b/solution.py
@@ -57,14 +57,21 @@
     rs_send,
     rs_recv,
     own,
-    x_ext,
-    cot_ext,
+    x_wide,
+    cot_wide,
+    x_tall,
+    cot_tall,
+    grad_tall,
+    out_tall,
+    first_tall,
+    last_tall,
     edge_send,
     edge_recv,
     cot_send,
     cot_recv,
     masks,
     tap_box,
+    tap_sums,
     gathered,
     piece,
     grad_act,
@@ -82,7 +89,8 @@
     length, depth = frames.shape
     width = taps.shape[1]
     hid = w_up_t.shape[0]
-    ext = length + 2 * LANES
+    side_length = length // 2
+    ext = side_length + 2 * LANES
     seq, ten = lax.axis_index("seq"), lax.axis_index("tensor")
     y, w = lax.div(seq, NW), lax.rem(seq, NW)
     core, x, z = lax.rem(ten, 2), lax.rem(lax.div(ten, 2), NX), lax.div(ten, 2 * NX)
@@ -160,7 +168,6 @@
     act[...] = up
     sig[...] = gate
     hidden[...] = (up * gate).astype(BF16)
-    cot_ext[:, LANES : LANES + length] = cot_t[...].astype(F32)
     cot_send[0] = cot_t[:, length - LANES :]
     cot_send[1] = cot_t[:, :LANES]
 
@@ -205,6 +212,21 @@
         == ten * width + lax.broadcasted_iota(jnp.int32, (width, depth), 0)
     ).astype(BF16)
     own[...] = dot(pick, frames[...], 1, 1)
+    def place(wide, block, value):
+        if block <= ext // LANES - 2:
+            wide[0:width, (block + 1) * LANES : (block + 2) * LANES] = value
+        shifted = block - side_length // LANES
+        if shifted >= -1:
+            wide[64 : 64 + width, (shifted + 1) * LANES : (shifted + 2) * LANES] = value
+
+    def turn_round(wide, tall):
+        for low in range(0, ext, LANES):
+            tall[low : low + LANES, :] = wide[:, low : low + LANES].T
+
+    x_wide[...] = jnp.zeros_like(x_wide)
+    cot_wide[...] = jnp.zeros_like(cot_wide)
+    for block in range(chunks):
+        place(cot_wide, block, cot_t[:, block * LANES : (block + 1) * LANES].astype(F32))
     limits = bounds[...]
     limits = jnp.concatenate(
         [
@@ -214,15 +236,28 @@
         ],
         axis=1,
     )
-    lower = jnp.broadcast_to(limits[0:1, :], (8, ext))
-    upper = jnp.broadcast_to(limits[1:2, :], (8, ext))
-    spots = seq * length - LANES + lax.broadcasted_iota(jnp.int32, (8, ext), 1)
-    for tap in range(K):
-        target = spots + (tap - HALF)
-        masks[tap] = jnp.where((target >= lower) & (target < upper), 1.0, 0.0).astype(F32)
-    tap_box[...] = jnp.zeros((LANES, LANES), F32)
+    spots = seq * length - LANES + lax.broadcasted_iota(jnp.int32, limits.shape, 1)
+    limits = (limits - spots).astype(F32)
+    for row, tall in ((0, first_tall), (1, last_tall)):
+        for low in range(0, ext, LANES):
+            tall[low : low + LANES, :] = jnp.concatenate(
+                [
+                    jnp.broadcast_to(limits[row : row + 1, low + i : low + i + LANES], (64, LANES))
+                    for i in (0, side_length)
+                ],
+                axis=0,
+            ).T
+    first_row, last_row = LANES - 16, LANES + side_length + 16
+    for low in range(first_row, last_row, 32):
+        lowest, highest = first_tall[low : low + 32, :], last_tall[low : low + 32, :]
+        for tap in range(K):
+            offset = float(tap - HALF)
+            masks[tap, low - first_row : low - first_row + 32, :] = jnp.where(
+                (lowest <= offset) & (highest > offset), 1.0, 0.0
+            ).astype(F32)
+    tap_box[...] = jnp.zeros_like(tap_box)
     tap_box[0:K, 0:width] = taps[...]
-    tap_box[...] = tap_box[...].T
+    tap_box[...] = tap_box[...] + pltpu.roll(tap_box[...], 64, 1)
 
     edges = {}
 
@@ -243,7 +278,7 @@
         columns = slice(chunk * LANES, (chunk + 1) * LANES)
         branch = keep[chunk, 0:rows, :] + rs_recv[chunk, low : low + rows, :].astype(F32)
         mixed = (own[:, columns] + 0.5 * branch).astype(BF16)
-        x_ext[:, (chunk + 1) * LANES : (chunk + 2) * LANES] = mixed.astype(F32)
+        place(x_wide, chunk, mixed.astype(F32))
         if chunk == 0:
             edge_send[1] = mixed
             edges[1] = send(edge_send.at[1], edge_recv.at[1], before)
@@ -257,61 +292,74 @@
                 for chunk, way in units[turn - stage]:
                     rs_finish(stage, chunk, way)
 
-    for side, low in ((0, 0), (1, ext - LANES)):
+    for side, block in ((0, -1), (1, chunks)):
         cot_copies[side].wait_recv()
-        cot_ext[:, low : low + LANES] = cot_recv[side].astype(F32)
-    for side, low in ((0, 0), (1, ext - LANES)):
+        place(cot_wide, block, cot_recv[side].astype(F32))
+    turn_round(cot_wide, cot_tall)
+    for side, block in ((0, -1), (1, chunks)):
         edges[side].wait_recv()
-        x_ext[:, low : low + LANES] = edge_recv[side].astype(F32)
-
-    lane = lax.broadcasted_iota(jnp.int32, (8, LANES), 1)
-    groups = width // 16
-    columns_of = (slice(0, length // 2), slice(length // 2, length))
-    inner = slice(LANES, LANES + length)
-
-    def convolve(group):
-        rows = pl.ds(pl.multiple_of(group * 8, 8), 8)
-        here = x_ext[rows, :]
-        cot_here = cot_ext[rows, :]
-        tap_here = tap_box[rows, :]
-        conv = jnp.zeros((8, ext), F32)
+        place(x_wide, block, edge_recv[side].astype(F32))
+    turn_round(x_wide, x_tall)
+
+    spans = side_length // LANES
+    step = 104
+    for low in range(first_row, last_row, step):
+        here = x_tall[low : low + step, :]
+        conv = jnp.zeros((step, LANES), F32)
         for tap in range(K):
-            moved = pltpu.roll(here, (HALF - tap) % ext, 1) if tap != HALF else here
-            conv = conv + tap_here[:, tap : tap + 1] * (moved * masks[tap])
-        conv_sig = jax.nn.sigmoid(conv)
-        grad = cot_here * conv_sig * (1.0 + conv * (1.0 - conv_sig))
-        output = (here + conv * conv_sig)[:, inner]
-        total = cot_here
-        sums = jnp.zeros((8, LANES), F32)
-        here = here[:, inner]
-        for tap in range(K):
-            moved = pltpu.roll(grad, (tap - HALF) % ext, 1) if tap != HALF else grad
-            moved = moved * masks[K - 1 - tap]
-            total = total + tap_here[:, tap : tap + 1] * moved
-            term = jnp.sum(moved[:, inner] * here, axis=1, keepdims=True)
-            sums = jnp.where(lane == tap, term, sums)
-        kernel_ring[y, rows, :] = sums
-        return output, total[:, inner]
+            moved = x_tall[low + tap - HALF : low + tap - HALF + step, :]
+            mask = masks[tap, low - first_row : low - first_row + step, :]
+            conv = conv + tap_box[tap : tap + 1, :] * (moved * mask)
+        gate = jax.nn.sigmoid(conv)
+        grad_tall[low : low + step, :] = (
+            cot_tall[low : low + step, :] * gate * (1.0 + conv * (1.0 - gate))
+        )
+        out_tall[low : low + step, :] = here + conv * gate
+
+    def convolve_back(unit):
+        parts = []
+        step = LANES // 2
+        for low in range(LANES * (unit + 1), LANES * (unit + 2), step):
+            here = x_tall[low : low + step, :]
+            total = cot_tall[low : low + step, :]
+            for tap in range(K):
+                moved = grad_tall[low + HALF - tap : low + HALF - tap + step, :]
+                moved = moved * masks[K - 1 - tap, low - first_row : low - first_row + step, :]
+                total = total + tap_box[tap : tap + 1, :] * moved
+                term = jnp.sum((moved * here).reshape(step // 8, 8, LANES), axis=0)
+                if low == LANES:
+                    tap_sums[tap] = term
+                else:
+                    tap_sums[tap] = tap_sums[tap] + term
+            parts.append(total)
+        return jnp.concatenate(parts, axis=0).T
 
     ag = {}
 
     def ag_start(stage, unit, way):
         first, second = WAYS[way]
         target = (z_way(first), z_way(second), x_way(first), x_way(second), sibling)[stage]
-        rows = 16 << stage
+        rows = width << stage
         return send(
             gathered.at[unit, way, pl.ds(0, rows), :],
             gathered.at[unit, way, pl.ds(rows, rows), :],
             target,
         )
 
-    for unit in range(groups):
-        parts = [convolve(2 * unit), convolve(2 * unit + 1)]
-        output, grad_mixed = (jnp.concatenate(pair, axis=0) for pair in zip(*parts))
-        out_t[16 * unit : 16 * unit + 16, :] = output.astype(BF16)
+    for unit in range(spans):
+        grad_mixed = convolve_back(unit).astype(BF16)
         for way in range(2):
-            gathered[unit, way, 0:16, :] = grad_mixed[:, columns_of[way]].astype(BF16)
+            gathered[unit, way, 0:width, :] = grad_mixed[64 * way : 64 * way + width, :]
             ag[0, unit, way] = ag_start(0, unit, way)
+    for unit in range(spans):
+        output = out_tall[LANES * (unit + 1) : LANES * (unit + 2), :].T.astype(BF16)
+        for way in range(2):
+            left = side_length * way + LANES * unit
+            out_t[:, left : left + LANES] = output[64 * way : 64 * way + width, :]
+    tap_sums[K] = jnp.zeros((8, LANES), F32)
+    sums = jnp.sum(tap_sums[...], axis=1)
+    sums = sums + pltpu.roll(sums, 64, 1)
+    kernel_ring[y] = sums
 
     taps_flight = {}
 
@@ -344,14 +392,14 @@
                             1 - core if c else core,
                         )
                         spot = (c * NX + i) * NZ + j
+                        left = side_length * way + LANES * unit
                         piece[
-                            pl.ds(pl.multiple_of(home * width + 16 * unit, 16), 16),
-                            columns_of[way],
-                        ] = gathered[unit, way, spot * 16 : (spot + 1) * 16, :]
-
-    for turn in range(groups + 4):
+                            pl.ds(pl.multiple_of(home * width, 16), width), left : left + LANES
+                        ] = gathered[unit, way, spot * width : (spot + 1) * width, :]
+
+    for turn in range(spans + 4):
         for stage in range(5):
-            if 0 <= turn - stage < groups:
+            if 0 <= turn - stage < spans:
                 ag_finish(stage, turn - stage)
         if turn in (1, 2, 3):
             taps_wait(turn)
@@ -365,13 +413,15 @@
 
     tall, broad = hid // 2, depth // 4
 
-    def down_chunk(d):
-        low, left = tall * (d % 2), broad * (d // 2)
-        totals[0, d] = dot(hidden[low : low + tall, :], piece[left : left + broad, :], 1, 1)
-
-    def up_chunk(d):
-        low, left = tall * (d % 2), broad * (d // 2)
-        totals[1, d] = dot(grad_act[low : low + tall, :], normed[:, left : left + broad], 1, 0)
+    def down_chunks(i):
+        left = broad * i
+        product = dot(hidden[...], piece[left : left + broad, :], 1, 1)
+        totals[0, 2 * i], totals[0, 2 * i + 1] = product[:tall], product[tall:]
+
+    def up_chunks(i):
+        left = broad * i
+        product = dot(grad_act[...], normed[:, left : left + broad], 1, 0)
+        totals[1, 2 * i], totals[1, 2 * i + 1] = product[:tall], product[tall:]
 
     ring = {}
 
@@ -391,15 +441,15 @@
         ring_send[spot] = value.astype(BF16)
         ring[stream, side, k] = send(ring_send.at[spot], ring_recv.at[spot], y_way(step))
 
-    for d in range(8):
-        down_chunk(d)
+    for i in range(4):
+        down_chunks(i)
     ring_start(0, 0, 4)
     ring_start(0, 1, 3)
     grad_hidden = 0.5 * dot(w_down[...], piece[...], 1, 0)
     gate = sig[...]
     grad_act[...] = (grad_hidden * gate * (1.0 + act[...] * (1.0 - gate))).astype(BF16)
-    for d in range(8):
-        up_chunk(d)
+    for i in range(4):
+        up_chunks(i)
     ring_start(1, 1, 4)
     ring_start(1, 0, 3)
     ring_start(0, 0, 3)
@@ -431,8 +481,8 @@
     for copy in cross:
         copy.wait_recv()
     scale = 1.0 / math.sqrt(length * count)
-    tap_box[0:width, :] = (kernel_cross[0] + kernel_cross[1] + kernel_cross[2]) * scale
-    kernel_sum[...] = tap_box[...].T[0:K, 0:width]
+    summed = (kernel_cross[0] + kernel_cross[1] + kernel_cross[2]) * scale
+    kernel_sum[...] = summed[0:K, 0:width]
     mine = pl.ds(pl.multiple_of(w * third, third), third)
     share = {}
     for stream in range(2):
@@ -472,7 +522,7 @@
     length, depth = frames.shape
     width = taps.shape[1]
     hid = w_up.shape[1]
-    ext = length + 2 * LANES
+    ext = length // 2 + 2 * LANES
     chunks = length // LANES
     rs_rows = depth // 2 + depth // 4 + depth // 8 + depth // 16 + depth // 32
     block = (hid // 2, depth // 4)
@@ -497,15 +547,22 @@
             pltpu.VMEM((chunks, rs_rows, LANES), BF16),
             pltpu.VMEM((chunks, rs_rows, LANES), BF16),
             pltpu.VMEM((width, length), F32),
-            pltpu.VMEM((width, ext), F32),
-            pltpu.VMEM((width, ext), F32),
+            pltpu.VMEM((LANES, ext), F32),
+            pltpu.VMEM((LANES, ext), F32),
+            pltpu.VMEM((ext, LANES), F32),
+            pltpu.VMEM((ext, LANES), F32),
+            pltpu.VMEM((ext, LANES), F32),
+            pltpu.VMEM((ext, LANES), F32),
+            pltpu.VMEM((ext, LANES), F32),
+            pltpu.VMEM((ext, LANES), F32),
             pltpu.VMEM((2, width, LANES), BF16),
             pltpu.VMEM((2, width, LANES), BF16),
             pltpu.VMEM((2, width, LANES), BF16),
             pltpu.VMEM((2, width, LANES), BF16),
-            pltpu.VMEM((K, 8, ext), F32),
-            pltpu.VMEM((LANES, LANES), F32),
-            pltpu.VMEM((width // 16, 2, depth // width * 16, length // 2), BF16),
+            pltpu.VMEM((K, length // 2 + 32, LANES), F32),
+            pltpu.VMEM((K + 1, LANES), F32),
+            pltpu.VMEM((K + 1, 8, LANES), F32),
+            pltpu.VMEM((chunks // 2, 2, depth, LANES), BF16),
             pltpu.VMEM((depth, length), BF16),
             pltpu.VMEM((hid, length), BF16),
             pltpu.VMEM((2, NY, *block), F32),
@@ -514,8 +571,8 @@
             pltpu.VMEM((4, block[0] // NW, block[1]), BF16),
             pltpu.VMEM((4, block[0] // NW, block[1]), BF16),
             pltpu.VMEM((2, NY, *block), BF16),
-            pltpu.VMEM((NY, width, LANES), F32),
-            pltpu.VMEM((NW, width, LANES), F32),
+            pltpu.VMEM((NY, K + 1, LANES), F32),
+            pltpu.VMEM((NW, K + 1, LANES), F32),
             pltpu.SemaphoreType.DMA((COPIES,)),
             pltpu.SemaphoreType.DMA((COPIES,)),
         ],

time: 128 us -> 120 us (0.938)
  the two profiles are of different devices: /device:TPU:2 before, /device:TPU:8 now
where the time goes in v3:
time: 120 us
  Pallas kernels  115 us (96%)
  other arithmetic  2.98 us (2%)
  local copies, waits for them, and re-layouts  1.25 us (1%)
    pallas_call x1, Pallas kernels, body(): pl.pallas_call(kernel, out_shape=(jax.ShapeDtypeStruct((width, length), B...  115 us
    mul x1, other arithmetic, body(): grads[0].astype(F32) * (0.5 * scale)  2.98 us

profile of v3, /device:TPU:8, one launch (start us, length us, event | category | flops | bytes accessed | tf_op | source)
XLA Modules:
  0.0 120.1 jit_solution(6632913918655953393)
XLA Ops:
  0.6 115.2 %shard_map.93 = (bf16[48,768]{1,0:T(8,128)(2,1)}, f32[31,48]{1,0:T(8,128)}, bf16[2,192,1536]{2,1,0:T(8,128)(2,1)}) custom-call(bf16[768,1536]{1,0:T(8,128)(2,1)} %frames.1, bf16[192,1536]{1,0:T(8,128)(2,1)} %bitcast.9, bf16[192,1536]{1,0:T(8,128)(2,1)} %w_down.1, f32[31,48]{1,0:T(8,128)} %taps.1, s32[2,768]{1,0:T(2,128)} %bounds.1, bf16[48,768]{1,0:T(8,128)(2,1)} %bitcast.11), custom_call_target="tpu_custom_call" | custom-call | tf_op jit(solution)/shard_map/pallas_call | solution.py:530
  115.8 0.0 copy-start
  115.8 0.0 copy-start.1
  115.8 3.0 %multiply_bitcast_fusion = (f32[192,1536]{1,0:T(8,128)}, f32[1536,192]{0,1:T(8,128)}) fusion(bf16[2,192,1536]{2,1,0:T(8,128)(2,1)} %get-tuple-element.8), kind=kLoop, calls=%fused_computation | loop fusion | flops 1179648 | bytes 3538944 | tf_op jit(solution)/shard_map/mul | solution.py:584
  118.8 0.0 copy-done
  118.8 0.6 copy.12
  119.5 0.0 copy-done.1
  119.5 0.6 copy.13
Async XLA Ops:
  115.8 3.0 %copy-start = (bf16[48,768]{1,0:T(8,128)(2,1)S(1)}, bf16[48,768]{1,0:T(8,128)(2,1)}, u32[]{:S(2)}) copy-start(bf16[48,768]{1,0:T(8,128)(2,1)} %get-tuple-element.7) | copy-start | bytes 221188
  115.8 3.6 %copy-start.1 = (f32[31,48]{1,0:T(8,128)S(1)}, f32[31,48]{1,0:T(8,128)}, u32[]{:S(2)}) copy-start(f32[31,48]{1,0:T(8,128)} %get-tuple-element.19) | copy-start | bytes 17860

commit v4 on v3

--- a/solution.py
+++ b/solution.py
@@ -1,4 +1,5 @@
 import math
+from functools import partial
 
 import jax
 import jax.numpy as jnp
@@ -14,7 +15,7 @@
 LANES = 128
 WAYS = ((1, 3), (3, 1))
 HOPS = ((4, 3), (3, 4))
-COPIES = 109
+COPIES = 137
 F32, BF16 = jnp.float32, jnp.bfloat16
 
 
@@ -137,18 +138,6 @@
         started.append(copy)
         return copy
 
-    block = LANES
-
-    def normalise(i, carry):
-        rows = pl.ds(pl.multiple_of(i * block, block), block)
-        wide = frames[rows, :].astype(F32)
-        mean = jnp.mean(wide, axis=1, keepdims=True)
-        centred = wide - mean
-        var = jnp.mean(centred * centred, axis=1, keepdims=True)
-        normed[rows, :] = (centred / jnp.sqrt(var + 1e-05)).astype(BF16)
-        return carry
-
-    lax.fori_loop(0, length // block, normalise, 0)
     w_down_t[...] = w_down[...].astype(F32).T.astype(BF16)
     for way in range(2):
         for c in range(2):
@@ -163,15 +152,8 @@
                     ordered[way, spot * width : (spot + 1) * width, :] = w_down_t[
                         pl.ds(pl.multiple_of(home * width, 16), width), :
                     ]
-    up = dot(w_up_t[...], normed[...], 1, 1)
-    gate = jax.nn.sigmoid(up)
-    act[...] = up
-    sig[...] = gate
-    hidden[...] = (up * gate).astype(BF16)
     cot_send[0] = cot_t[:, length - LANES :]
     cot_send[1] = cot_t[:, :LANES]
-
-    pl.semaphore_wait(barrier, len(partners))
 
     half = depth // 2
     starts, height = [], half
@@ -192,26 +174,9 @@
         )
 
     flights = {}
-    for unit in units:
-        for chunk, way in unit:
-            columns = slice(chunk * LANES, (chunk + 1) * LANES)
-            part = hidden[:, columns]
-            rs_send[chunk, 0:half, :] = dot(ordered[way, half:, :], part, 1, 0).astype(BF16)
-            flights[0, chunk] = rs_start(0, chunk, way)
-        for chunk, way in unit:
-            columns = slice(chunk * LANES, (chunk + 1) * LANES)
-            keep[chunk] = dot(ordered[way, :half, :], hidden[:, columns], 1, 0)
-
-    cot_copies = [
-        send(cot_send.at[0], cot_recv.at[0], after),
-        send(cot_send.at[1], cot_recv.at[1], before),
-    ]
-
-    pick = (
-        lax.broadcasted_iota(jnp.int32, (width, depth), 1)
-        == ten * width + lax.broadcasted_iota(jnp.int32, (width, depth), 0)
-    ).astype(BF16)
-    own[...] = dot(pick, frames[...], 1, 1)
+    cot_copies = []
+    first_row, last_row = LANES - 16, LANES + side_length + 16
+
     def place(wide, block, value):
         if block <= ext // LANES - 2:
             wide[0:width, (block + 1) * LANES : (block + 2) * LANES] = value
@@ -223,41 +188,77 @@
         for low in range(0, ext, LANES):
             tall[low : low + LANES, :] = wide[:, low : low + LANES].T
 
-    x_wide[...] = jnp.zeros_like(x_wide)
-    cot_wide[...] = jnp.zeros_like(cot_wide)
-    for block in range(chunks):
-        place(cot_wide, block, cot_t[:, block * LANES : (block + 1) * LANES].astype(F32))
-    limits = bounds[...]
-    limits = jnp.concatenate(
-        [
-            jnp.broadcast_to(limits[:, :1], (2, LANES)),
-            limits,
-            jnp.broadcast_to(limits[:, length - 1 :], (2, LANES)),
-        ],
-        axis=1,
-    )
-    spots = seq * length - LANES + lax.broadcasted_iota(jnp.int32, limits.shape, 1)
-    limits = (limits - spots).astype(F32)
-    for row, tall in ((0, first_tall), (1, last_tall)):
-        for low in range(0, ext, LANES):
-            tall[low : low + LANES, :] = jnp.concatenate(
-                [
-                    jnp.broadcast_to(limits[row : row + 1, low + i : low + i + LANES], (64, LANES))
-                    for i in (0, side_length)
-                ],
-                axis=0,
-            ).T
-    first_row, last_row = LANES - 16, LANES + side_length + 16
-    for low in range(first_row, last_row, 32):
-        lowest, highest = first_tall[low : low + 32, :], last_tall[low : low + 32, :]
-        for tap in range(K):
-            offset = float(tap - HALF)
-            masks[tap, low - first_row : low - first_row + 32, :] = jnp.where(
-                (lowest <= offset) & (highest > offset), 1.0, 0.0
-            ).astype(F32)
-    tap_box[...] = jnp.zeros_like(tap_box)
-    tap_box[0:K, 0:width] = taps[...]
-    tap_box[...] = tap_box[...] + pltpu.roll(tap_box[...], 64, 1)
+    def hidden_chunk(chunk):
+        rows = slice(chunk * LANES, (chunk + 1) * LANES)
+        wide = frames[rows, :].astype(F32)
+        mean = jnp.mean(wide, axis=1, keepdims=True)
+        centred = wide - mean
+        var = jnp.mean(centred * centred, axis=1, keepdims=True)
+        normed[rows, :] = (centred / jnp.sqrt(var + 1e-05)).astype(BF16)
+        up = dot(w_up_t[...], normed[rows, :], 1, 1)
+        gate = jax.nn.sigmoid(up)
+        act[:, rows] = up
+        sig[:, rows] = gate
+        hidden[:, rows] = (up * gate).astype(BF16)
+
+    def rs_begin(turn):
+        unit = units[turn]
+        for chunk, _ in unit:
+            hidden_chunk(chunk)
+        if turn == 0:
+            pl.semaphore_wait(barrier, len(partners))
+        for chunk, way in unit:
+            part = hidden[:, chunk * LANES : (chunk + 1) * LANES]
+            rs_send[chunk, 0:half, :] = dot(ordered[way, half:, :], part, 1, 0).astype(BF16)
+            flights[0, chunk] = rs_start(0, chunk, way)
+        for chunk, way in unit:
+            part = hidden[:, chunk * LANES : (chunk + 1) * LANES]
+            keep[chunk] = dot(ordered[way, :half, :], part, 1, 0)
+
+    def prepare_masks():
+        limits = bounds[...]
+        limits = jnp.concatenate(
+            [
+                jnp.broadcast_to(limits[:, :1], (2, LANES)),
+                limits,
+                jnp.broadcast_to(limits[:, length - 1 :], (2, LANES)),
+            ],
+            axis=1,
+        )
+        spots = seq * length - LANES + lax.broadcasted_iota(jnp.int32, limits.shape, 1)
+        limits = (limits - spots).astype(F32)
+        for row, tall in ((0, first_tall), (1, last_tall)):
+            for low in range(0, ext, LANES):
+                tall[low : low + LANES, :] = jnp.concatenate(
+                    [
+                        jnp.broadcast_to(limits[row : row + 1, low + i : low + i + LANES], (64, LANES))
+                        for i in (0, side_length)
+                    ],
+                    axis=0,
+                ).T
+        for low in range(first_row, last_row, 32):
+            lowest, highest = first_tall[low : low + 32, :], last_tall[low : low + 32, :]
+            for tap in range(K):
+                offset = float(tap - HALF)
+                masks[tap, low - first_row : low - first_row + 32, :] = jnp.where(
+                    (lowest <= offset) & (highest > offset), 1.0, 0.0
+                ).astype(F32)
+
+    def prepare_taps():
+        x_wide[...] = jnp.zeros_like(x_wide)
+        cot_wide[...] = jnp.zeros_like(cot_wide)
+        for block in range(chunks):
+            place(cot_wide, block, cot_t[:, block * LANES : (block + 1) * LANES].astype(F32))
+        tap_box[...] = jnp.zeros_like(tap_box)
+        tap_box[0:K, 0:width] = taps[...]
+        tap_box[...] = tap_box[...] + pltpu.roll(tap_box[...], 64, 1)
+
+    def prepare_own():
+        pick = (
+            lax.broadcasted_iota(jnp.int32, (width, depth), 1)
+            == ten * width + lax.broadcasted_iota(jnp.int32, (width, depth), 0)
+        ).astype(BF16)
+        own[...] = dot(pick, frames[...], 1, 1)
 
     edges = {}
 
@@ -286,11 +287,21 @@
             edge_send[0] = mixed
             edges[0] = send(edge_send.at[0], edge_recv.at[0], after)
 
-    for turn in range(len(units) + 4):
+    for turn in range(len(units) + 5):
+        if turn < len(units):
+            rs_begin(turn)
         for stage in range(5):
-            if 0 <= turn - stage < len(units):
-                for chunk, way in units[turn - stage]:
+            if 0 <= turn - 1 - stage < len(units):
+                for chunk, way in units[turn - 1 - stage]:
                     rs_finish(stage, chunk, way)
+        if turn == 1:
+            cot_copies.append(send(cot_send.at[0], cot_recv.at[0], after))
+            cot_copies.append(send(cot_send.at[1], cot_recv.at[1], before))
+            prepare_taps()
+        if turn == 2:
+            prepare_own()
+        if turn == 3:
+            prepare_masks()
 
     for side, block in ((0, -1), (1, chunks)):
         cot_copies[side].wait_recv()
@@ -497,25 +508,35 @@
             )
     spread = {}
     for k in range(1, 6):
-        for stream in range(2):
-            if k == 1:
-                for step in (1, 2):
-                    share[stream, step].wait_recv()
-            for side in range(2):
-                step = (1, -1)[side]
-                if 1 < k <= HOPS[stream][side] + 1:
-                    spread[stream, side, k - 1].wait_recv()
-                if k <= HOPS[stream][side]:
-                    spot = lax.rem(y + NY - step * (k - 1), NY)
-                    spread[stream, side, k] = send(
-                        whole.at[stream, spot], whole.at[stream, spot], y_way(step)
-                    )
+        for part in range(NW):
+            rows = pl.ds(pl.multiple_of(lax.rem(w + NW - part, NW) * third, third), third)
+            for stream in range(2):
+                if k == 1 and part > 0:
+                    share[stream, part].wait_recv()
+                for side in range(2):
+                    step = (1, -1)[side]
+                    if 1 < k <= HOPS[stream][side] + 1:
+                        spread[stream, side, k - 1, part].wait_recv()
+                    if k <= HOPS[stream][side]:
+                        spot = lax.rem(y + NY - step * (k - 1), NY)
+                        spread[stream, side, k, part] = send(
+                            whole.at[stream, spot, rows, :],
+                            whole.at[stream, spot, rows, :],
+                            y_way(step),
+                        )
     for stream in range(2):
         for d in range(8):
             low, left = tall * (d % 2), broad * (d // 2)
             grads[stream, low : low + tall, left : left + broad] = whole[stream, d]
     for copy in started:
         copy.wait_send()
+
+
+def finish(scale, grads, out_t, kernel_sum, down, up_t, out, kernel_out):
+    down[...] = grads[0].astype(F32) * (0.5 * scale)
+    up_t[...] = grads[1].astype(F32) * scale
+    out[...] = out_t[...]
+    kernel_out[...] = kernel_sum[...]
 
 
 def body(frames, w_up, w_down, taps, bounds, cot):
@@ -581,8 +602,27 @@
         ),
     )(frames, w_up.T, w_down, taps, bounds, cot.T)
     scale = 1.0 / math.sqrt(length * NY * NW)
-    down, up = grads[0].astype(F32) * (0.5 * scale), grads[1].astype(F32) * scale
-    return out_t.T, up.T, down, kernel_sum
+    steps = 4
+    rows = pl.BlockSpec((hid // steps, depth), lambda i: (i, 0))
+    out_all = pl.BlockSpec((width, length), lambda i: (0, 0))
+    taps_all = pl.BlockSpec((K, width), lambda i: (0, 0))
+    down, up_t, out_t, kernel_sum = pl.pallas_call(
+        partial(finish, scale),
+        grid=(steps,),
+        out_shape=(
+            jax.ShapeDtypeStruct((hid, depth), F32),
+            jax.ShapeDtypeStruct((hid, depth), F32),
+            jax.ShapeDtypeStruct((width, length), BF16),
+            jax.ShapeDtypeStruct((K, width), F32),
+        ),
+        in_specs=[
+            pl.BlockSpec((2, hid // steps, depth), lambda i: (0, i, 0)),
+            out_all,
+            taps_all,
+        ],
+        out_specs=(rows, rows, out_all, taps_all),
+    )(grads, out_t, kernel_sum)
+    return out_t.T, up_t.T, down, kernel_sum
 
 
 def solution(mesh):

time: 120 us -> 116 us (0.967)
  the two profiles are of different devices: /device:TPU:8 before, /device:TPU:16 now
where the time goes in v4:
time: 116 us
  Pallas kernels  115 us (99%)
    pallas_call x1, Pallas kernels, body(): pl.pallas_call(kernel, out_shape=(jax.ShapeDtypeStruct((width, length), B...  111 us
    pallas_call x1, Pallas kernels, body(): pl.pallas_call(partial(finish, scale), grid=(steps,), out_shape=(jax.Shap...  3.7 us

profile of v4, /device:TPU:16, one launch (start us, length us, event | category | flops | bytes accessed | tf_op | source)
XLA Modules:
  0.0 115.7 jit_solution(7955957464502099046)
XLA Ops:
  0.6 111.4 %shard_map.93 = (bf16[48,768]{1,0:T(8,128)(2,1)}, f32[31,48]{1,0:T(8,128)}, bf16[2,192,1536]{2,1,0:T(8,128)(2,1)}) custom-call(bf16[768,1536]{1,0:T(8,128)(2,1)} %frames.1, bf16[192,1536]{1,0:T(8,128)(2,1)} %bitcast.4, bf16[192,1536]{1,0:T(8,128)(2,1)} %w_down.1, f32[31,48]{1,0:T(8,128)} %taps.1, s32[2,768]{1,0:T(2,128)} %bounds.1, bf16[48,768]{1,0:T(8,128)(2,1)} %bitcast.5), custom_call_target="tpu_custom_call" | custom-call | tf_op jit(solution)/shard_map/pallas_call | solution.py:551
  112.0 3.7 %shard_map.94 = (f32[192,1536]{1,0:T(8,128)}, f32[192,1536]{1,0:T(8,128)}, bf16[48,768]{1,0:T(8,128)(2,1)}, f32[31,48]{1,0:T(8,128)}) custom-call(bf16[2,192,1536]{2,1,0:T(8,128)(2,1)} %get-tuple-element.11.grads, bf16[48,768]{1,0:T(8,128)(2,1)} %get-tuple-element.12.out_t, f32[31,48]{1,0:T(8,128)} %get-tuple-element.13.kernel_sum), custom_call_target="tpu_custom_call" | custom-call | tf_op jit(solution)/shard_map/pallas_call | solution.py:609

commit v5 on v4

--- a/solution.py
+++ b/solution.py
@@ -15,7 +15,7 @@
 LANES = 128
 WAYS = ((1, 3), (3, 1))
 HOPS = ((4, 3), (3, 4))
-COPIES = 137
+COPIES = 143
 F32, BF16 = jnp.float32, jnp.bfloat16
 
 
@@ -75,7 +75,6 @@
     tap_sums,
     gathered,
     piece,
-    grad_act,
     totals,
     ring_send,
     ring_recv,
@@ -349,19 +348,21 @@
 
     def ag_start(stage, unit, way):
         first, second = WAYS[way]
-        target = (z_way(first), z_way(second), x_way(first), x_way(second), sibling)[stage]
-        rows = width << stage
-        return send(
-            gathered.at[unit, way, pl.ds(0, rows), :],
-            gathered.at[unit, way, pl.ds(rows, rows), :],
-            target,
+        targets = (z_way(first), z_way(second), x_way(first), x_way(second), sibling, sibling)
+        low, rows, move = 0, width << stage, width << stage
+        if stage >= 4:
+            low, rows, move = (0, half // 2, half) if stage == 4 else (half // 2, half // 2, half)
+        ag[stage, unit, way] = send(
+            gathered.at[unit, way, pl.ds(low, rows), :],
+            gathered.at[unit, way, pl.ds(low + move, rows), :],
+            targets[stage],
         )
 
     for unit in range(spans):
         grad_mixed = convolve_back(unit).astype(BF16)
         for way in range(2):
             gathered[unit, way, 0:width, :] = grad_mixed[64 * way : 64 * way + width, :]
-            ag[0, unit, way] = ag_start(0, unit, way)
+            ag_start(0, unit, way)
     for unit in range(spans):
         output = out_tall[LANES * (unit + 1) : LANES * (unit + 2), :].T.astype(BF16)
         for way in range(2):
@@ -388,52 +389,76 @@
 
     taps_start(1)
 
+    def settle(unit, way, c):
+        for i in range(NX):
+            for j in range(NZ):
+                home = tensor_at(
+                    flip(z, relative(j, way)),
+                    flip(x, relative(i, way)),
+                    1 - core if c else core,
+                )
+                spot = (c * NX + i) * NZ + j
+                piece[
+                    unit,
+                    pl.ds(pl.multiple_of(home * width, 16), width),
+                    way * LANES : (way + 1) * LANES,
+                ] = gathered[unit, way, spot * width : (spot + 1) * width, :]
+
     def ag_finish(stage, unit):
         for way in range(2):
             ag[stage, unit, way].wait_recv()
-            if stage < 4:
-                ag[stage + 1, unit, way] = ag_start(stage + 1, unit, way)
-                continue
-            for c in range(2):
-                for i in range(NX):
-                    for j in range(NZ):
-                        home = tensor_at(
-                            flip(z, relative(j, way)),
-                            flip(x, relative(i, way)),
-                            1 - core if c else core,
-                        )
-                        spot = (c * NX + i) * NZ + j
-                        left = side_length * way + LANES * unit
-                        piece[
-                            pl.ds(pl.multiple_of(home * width, 16), width), left : left + LANES
-                        ] = gathered[unit, way, spot * width : (spot + 1) * width, :]
+            if stage < 3:
+                ag_start(stage + 1, unit, way)
+            if stage == 2:
+                ag_start(4, unit, way)
+            if stage == 3:
+                ag_start(5, unit, way)
+        for way in range(2):
+            if stage == 3:
+                settle(unit, way, 0)
+            if stage == 4:
+                ag[5, unit, way].wait_recv()
+                settle(unit, way, 1)
+
+    tall, broad = hid // 2, depth // 4
+
+    def of_unit(array, unit, axis):
+        low = LANES * unit
+        spots = (slice(low, low + LANES), slice(side_length + low, side_length + low + LANES))
+        return jnp.concatenate(
+            [array[:, spot] if axis else array[spot, :] for spot in spots], axis=axis
+        )
+
+    def add_chunks(stream, unit, i, product):
+        for d, part in ((2 * i, product[:tall]), (2 * i + 1, product[tall:])):
+            totals[stream, d] = part if unit == 0 else totals[stream, d] + part
+
+    def down_part(unit):
+        left_side = of_unit(hidden, unit, 1)
+        for i in range(4):
+            rows = slice(broad * i, broad * (i + 1))
+            add_chunks(0, unit, i, dot(left_side, piece[unit, rows, :], 1, 1))
+
+    def up_part(unit):
+        grad_hidden = 0.5 * dot(w_down[...], piece[unit], 1, 0)
+        gate = of_unit(sig, unit, 1)
+        grad_act = grad_hidden * gate * (1.0 + of_unit(act, unit, 1) * (1.0 - gate))
+        grad_act = grad_act.astype(BF16)
+        right_side = of_unit(normed, unit, 0)
+        for i in range(4):
+            columns = slice(broad * i, broad * (i + 1))
+            add_chunks(1, unit, i, dot(grad_act, right_side[:, columns], 1, 0))
 
     for turn in range(spans + 4):
         for stage in range(5):
             if 0 <= turn - stage < spans:
                 ag_finish(stage, turn - stage)
-        if turn in (1, 2, 3):
-            taps_wait(turn)
-            taps_start(turn + 1)
-    taps_wait(4)
-    total = kernel_ring[0]
-    for i in range(1, NY):
-        total = total + kernel_ring[i]
-    kernel_cross[w] = total
-    cross = [send(kernel_cross.at[w], kernel_cross.at[w], w_way(step)) for step in (1, 2)]
-
-    tall, broad = hid // 2, depth // 4
-
-    def down_chunks(i):
-        left = broad * i
-        product = dot(hidden[...], piece[left : left + broad, :], 1, 1)
-        totals[0, 2 * i], totals[0, 2 * i + 1] = product[:tall], product[tall:]
-
-    def up_chunks(i):
-        left = broad * i
-        product = dot(grad_act[...], normed[:, left : left + broad], 1, 0)
-        totals[1, 2 * i], totals[1, 2 * i + 1] = product[:tall], product[tall:]
-
+        if 4 <= turn < spans + 3:
+            down_part(turn - 4)
+            up_part(turn - 4)
+        if turn in (3, 5):
+            taps_wait(turn // 2)
+            taps_start(turn // 2 + 1)
     ring = {}
 
     def ring_spot(stream, side, k):
@@ -452,19 +477,22 @@
         ring_send[spot] = value.astype(BF16)
         ring[stream, side, k] = send(ring_send.at[spot], ring_recv.at[spot], y_way(step))
 
-    for i in range(4):
-        down_chunks(i)
+    down_part(spans - 1)
     ring_start(0, 0, 4)
     ring_start(0, 1, 3)
-    grad_hidden = 0.5 * dot(w_down[...], piece[...], 1, 0)
-    gate = sig[...]
-    grad_act[...] = (grad_hidden * gate * (1.0 + act[...] * (1.0 - gate))).astype(BF16)
-    for i in range(4):
-        up_chunks(i)
+    taps_wait(3)
+    taps_start(4)
+    up_part(spans - 1)
     ring_start(1, 1, 4)
     ring_start(1, 0, 3)
     ring_start(0, 0, 3)
     ring_start(1, 1, 3)
+    taps_wait(4)
+    total = kernel_ring[0]
+    for i in range(1, NY):
+        total = total + kernel_ring[i]
+    kernel_cross[w] = total
+    cross = [send(kernel_cross.at[w], kernel_cross.at[w], w_way(step)) for step in (1, 2)]
     for k in (2, 1):
         ring_start(0, 1, k)
         ring_start(1, 0, k)
@@ -524,17 +552,14 @@
                             whole.at[stream, spot, rows, :],
                             y_way(step),
                         )
-    for stream in range(2):
-        for d in range(8):
-            low, left = tall * (d % 2), broad * (d // 2)
-            grads[stream, low : low + tall, left : left + broad] = whole[stream, d]
+    grads[...] = whole[...]
     for copy in started:
         copy.wait_send()
 
 
 def finish(scale, grads, out_t, kernel_sum, down, up_t, out, kernel_out):
-    down[...] = grads[0].astype(F32) * (0.5 * scale)
-    up_t[...] = grads[1].astype(F32) * scale
+    down[...] = grads[0].reshape(down.shape).astype(F32) * (0.5 * scale)
+    up_t[...] = grads[1].reshape(up_t.shape).astype(F32) * scale
     out[...] = out_t[...]
     kernel_out[...] = kernel_sum[...]
 
@@ -553,7 +578,7 @@
         out_shape=(
             jax.ShapeDtypeStruct((width, length), BF16),
             jax.ShapeDtypeStruct((K, width), F32),
-            jax.ShapeDtypeStruct((2, hid, depth), BF16),
+            jax.ShapeDtypeStruct((2, NY, *block), BF16),
         ),
         in_specs=[vmem] * 6,
         out_specs=(vmem,) * 3,
@@ -584,8 +609,7 @@
             pltpu.VMEM((K + 1, LANES), F32),
             pltpu.VMEM((K + 1, 8, LANES), F32),
             pltpu.VMEM((chunks // 2, 2, depth, LANES), BF16),
-            pltpu.VMEM((depth, length), BF16),
-            pltpu.VMEM((hid, length), BF16),
+            pltpu.VMEM((chunks // 2, depth, 2 * LANES), BF16),
             pltpu.VMEM((2, NY, *block), F32),
             pltpu.VMEM((16, *block), BF16),
             pltpu.VMEM((16, *block), BF16),
@@ -603,7 +627,7 @@
     )(frames, w_up.T, w_down, taps, bounds, cot.T)
     scale = 1.0 / math.sqrt(length * NY * NW)
     steps = 4
-    rows = pl.BlockSpec((hid // steps, depth), lambda i: (i, 0))
+    columns = pl.BlockSpec((hid, depth // steps), lambda i: (0, i))
     out_all = pl.BlockSpec((width, length), lambda i: (0, 0))
     taps_all = pl.BlockSpec((K, width), lambda i: (0, 0))
     down, up_t, out_t, kernel_sum = pl.pallas_call(
@@ -616,11 +640,11 @@
             jax.ShapeDtypeStruct((K, width), F32),
         ),
         in_specs=[
-            pl.BlockSpec((2, hid // steps, depth), lambda i: (0, i, 0)),
+            pl.BlockSpec((2, NY // steps, *block), lambda i: (0, i, 0, 0)),
             out_all,
             taps_all,
         ],
-        out_specs=(rows, rows, out_all, taps_all),
+        out_specs=(columns, columns, out_all, taps_all),
     )(grads, out_t, kernel_sum)
     return out_t.T, up_t.T, down, kernel_sum
 

time: 116 us -> 117 us (level)
  the two profiles are of different devices: /device:TPU:16 before, /device:TPU:2 now
where the time goes in v5:
time: 117 us; the launch traced here: 116 us
  Pallas kernels  116 us (99%)
    pallas_call x1, Pallas kernels, body(): pl.pallas_call(kernel, out_shape=(jax.ShapeDtypeStruct((width, length), B...  112 us
    pallas_call x1, Pallas kernels, body(): pl.pallas_call(partial(finish, scale), grid=(steps,), out_shape=(jax.Shap...  3.7 us

profile of v5, /device:TPU:2, one launch (start us, length us, event | category | flops | bytes accessed | tf_op | source)
XLA Modules:
  0.0 116.3 jit_solution(920079272183894867)
XLA Ops:
  0.6 111.9 %shard_map.93 = (bf16[48,768]{1,0:T(8,128)(2,1)}, f32[31,48]{1,0:T(8,128)}, bf16[2,8,96,384]{3,2,1,0:T(8,128)(2,1)}) custom-call(bf16[768,1536]{1,0:T(8,128)(2,1)} %frames.1, bf16[192,1536]{1,0:T(8,128)(2,1)} %bitcast.4, bf16[192,1536]{1,0:T(8,128)(2,1)} %w_down.1, f32[31,48]{1,0:T(8,128)} %taps.1, s32[2,768]{1,0:T(2,128)} %bounds.1, bf16[48,768]{1,0:T(8,128)(2,1)} %bitcast.5), custom_call_target="tpu_custom_call" | custom-call | tf_op jit(solution)/shard_map/pallas_call | solution.py:576
  112.6 3.7 %shard_map.94 = (f32[192,1536]{1,0:T(8,128)}, f32[192,1536]{1,0:T(8,128)}, bf16[48,768]{1,0:T(8,128)(2,1)}, f32[31,48]{1,0:T(8,128)}) custom-call(bf16[2,8,96,384]{3,2,1,0:T(8,128)(2,1)} %get-tuple-element.11.grads, bf16[48,768]{1,0:T(8,128)(2,1)} %get-tuple-element.12.out_t, f32[31,48]{1,0:T(8,128)} %get-tuple-element.13.kernel_sum), custom_call_target="tpu_custom_call" | custom-call | tf_op jit(solution)/shard_map/pallas_call | solution.py:633

commit v6 on v5

--- a/solution.py
+++ b/solution.py
@@ -313,7 +313,9 @@
 
     spans = side_length // LANES
     step = 104
-    for low in range(first_row, last_row, step):
+
+    def convolve(block):
+        low = first_row + step * block
         here = x_tall[low : low + step, :]
         conv = jnp.zeros((step, LANES), F32)
         for tap in range(K):
@@ -358,7 +360,9 @@
             targets[stage],
         )
 
+    convolve(0)
     for unit in range(spans):
+        convolve(unit + 1)
         grad_mixed = convolve_back(unit).astype(BF16)
         for way in range(2):
             gathered[unit, way, 0:width, :] = grad_mixed[64 * way : 64 * way + width, :]
@@ -558,8 +562,12 @@
 
 
 def finish(scale, grads, out_t, kernel_sum, down, up_t, out, kernel_out):
-    down[...] = grads[0].reshape(down.shape).astype(F32) * (0.5 * scale)
-    up_t[...] = grads[1].reshape(up_t.shape).astype(F32) * scale
+    hid, broad = down.shape[0], grads.shape[3]
+    for i in range(NY // 2):
+        columns = slice(broad * i, broad * (i + 1))
+        pair = slice(2 * i, 2 * i + 2)
+        down[:, columns] = grads[0, pair].reshape(hid, broad).astype(F32) * (0.5 * scale)
+        up_t[:, columns] = grads[1, pair].reshape(hid, broad).astype(F32) * scale
     out[...] = out_t[...]
     kernel_out[...] = kernel_sum[...]
 
@@ -626,25 +634,16 @@
         ),
     )(frames, w_up.T, w_down, taps, bounds, cot.T)
     scale = 1.0 / math.sqrt(length * NY * NW)
-    steps = 4
-    columns = pl.BlockSpec((hid, depth // steps), lambda i: (0, i))
-    out_all = pl.BlockSpec((width, length), lambda i: (0, 0))
-    taps_all = pl.BlockSpec((K, width), lambda i: (0, 0))
     down, up_t, out_t, kernel_sum = pl.pallas_call(
         partial(finish, scale),
-        grid=(steps,),
         out_shape=(
             jax.ShapeDtypeStruct((hid, depth), F32),
             jax.ShapeDtypeStruct((hid, depth), F32),
             jax.ShapeDtypeStruct((width, length), BF16),
             jax.ShapeDtypeStruct((K, width), F32),
         ),
-        in_specs=[
-            pl.BlockSpec((2, NY // steps, *block), lambda i: (0, i, 0, 0)),
-            out_all,
-            taps_all,
-        ],
-        out_specs=(columns, columns, out_all, taps_all),
+        in_specs=[vmem] * 3,
+        out_specs=(vmem,) * 4,
     )(grads, out_t, kernel_sum)
     return out_t.T, up_t.T, down, kernel_sum
 

time: 117 us -> 115 us (0.983)
  the two profiles are of different devices: /device:TPU:2 before, /device:TPU:10 now
where the time goes in v6:
time: 115 us
  Pallas kernels  114 us (99%)
    pallas_call x1, Pallas kernels, body(): pl.pallas_call(kernel, out_shape=(jax.ShapeDtypeStruct((width, length), B...  112 us
    pallas_call x1, Pallas kernels, body(): pl.pallas_call(partial(finish, scale), out_shape=(jax.ShapeDtypeStruct((h...  2.89 us

profile of v6, /device:TPU:10, one launch (start us, length us, event | category | flops | bytes accessed | tf_op | source)
XLA Modules:
  0.0 115.1 jit_solution(16066801626482299618)
XLA Ops:
  0.6 111.5 %shard_map.93 = (bf16[48,768]{1,0:T(8,128)(2,1)}, f32[31,48]{1,0:T(8,128)}, bf16[2,8,96,384]{3,2,1,0:T(8,128)(2,1)}) custom-call(bf16[768,1536]{1,0:T(8,128)(2,1)} %frames.1, bf16[192,1536]{1,0:T(8,128)(2,1)} %bitcast.4, bf16[192,1536]{1,0:T(8,128)(2,1)} %w_down.1, f32[31,48]{1,0:T(8,128)} %taps.1, s32[2,768]{1,0:T(2,128)} %bounds.1, bf16[48,768]{1,0:T(8,128)(2,1)} %bitcast.5), custom_call_target="tpu_custom_call" | custom-call | tf_op jit(solution)/shard_map/pallas_call | solution.py:584
  112.2 2.9 %shard_map.94 = (f32[192,1536]{1,0:T(8,128)}, f32[192,1536]{1,0:T(8,128)}, bf16[48,768]{1,0:T(8,128)(2,1)}, f32[31,48]{1,0:T(8,128)}) custom-call(bf16[2,8,96,384]{3,2,1,0:T(8,128)(2,1)} %get-tuple-element.11.grads, bf16[48,768]{1,0:T(8,128)(2,1)} %get-tuple-element.12.out_t, f32[31,48]{1,0:T(8,128)} %get-tuple-element.13.kernel_sum), custom_call_target="tpu_custom_call" | custom-call | tf_op jit(solution)/shard_map/pallas_call | solution.py:637
